TPU v7x, 1024 devices: a whole 4x4x32 slice. The times are simulated.
1024 devices in a mesh: row: 32 (over y, z_hi, core), col: 32 (over z_lo, x).
Axes of the slice: x: 4, y: 4, z: 32 (z_hi: 4, z_lo: 8; z = z_hi * 8 + z_lo), core: 2. Of those that a mesh axis runs over, the one named last changes fastest.
Arguments:
- a_blocks: bfloat16 [32, 32, 12, 128, 128], P('row', 'col'), may hold values from -6 to 6
- a_index: int32 [32, 32, 2, 12], P('row', 'col'), may hold values from 0 to 31, as said below
- a_count: int32 [32, 32], P('row', 'col'), may hold values from 6 to 12, as said below
- b_blocks: bfloat16 [1, 32, 32, 6, 128, 128], P(None, 'row', 'col'), may hold values from -0.5 to 0.5
- b_index: int32 [1, 32, 32, 2, 6], P(None, 'row', 'col'), may hold values from 0 to 31, as said below
- b_count: int32 [1, 32, 32], P(None, 'row', 'col'), may hold values from 3 to 6, as said below
Outputs:
- product: bfloat16 [32768, 16384], P('row', 'col')
Inputs may be any that keep to these rules, and one draw needn't show every extreme that they name: Within one panel the stored positions are distinct; a_index rows are below 8 and columns below 32. Within one panel the stored positions are distinct; b_index rows are below 32 and columns below 4. `a_count`: slots at or past the count are padding. `b_count`: slots at or past the count are padding.
All inputs are finite; a program needn't handle non-finite values.
Results may differ from a plain program's by a relative error of at most 0.001.
Values may be sent and summed in bfloat16 or wider, within the bound.
No kernel may reach another device: no remote copies, remote signals or barrier semaphores. Data moves between devices by JAX's collectives and lax.ppermute only.
A program may use at most 32 MiB of HBM per device.

v0:
```python
import jax
import jax.numpy as jnp
from jax import lax
from jax.sharding import PartitionSpec as P

BLOCK = 128
KR = 8
KC = 4
TICKS = 4


def for_sending(value):
    return jax.tree.map(lambda a: a.astype(jnp.bfloat16) if a.dtype == jnp.float32 else a, value)


def passed_along(block, axis, distance):
    devices = range(lax.axis_size(axis))
    route = [((i - distance) % len(devices), i) for i in devices]
    return lax.ppermute(block, axis, route)


def panel_product(a_blk, a_idx, a_cnt, b_blk, b_idx, b_cnt):
    slots_a = a_blk.shape[0]
    slots_b = b_blk.shape[0]
    side = a_blk.shape[-1]
    live_a = jnp.arange(slots_a, dtype=jnp.int32) < a_cnt[0]
    live_b = jnp.arange(slots_b, dtype=jnp.int32) < b_cnt[0]
    match = (a_idx[1][:, None] == b_idx[0][None, :]) & live_a[:, None] & live_b[None, :]
    place = b_idx[1][:, None] == jnp.arange(KC, dtype=jnp.int32)[None, :]
    select = (match[:, :, None] & place[None, :, :]).astype(jnp.bfloat16)
    strip = jnp.einsum("suc,uxy->sxcy", select, b_blk, preferred_element_type=jnp.float32)
    strip = strip.astype(jnp.bfloat16).reshape(slots_a, side, KC * side)
    prods = jnp.einsum("sxy,syz->sxz", a_blk, strip, preferred_element_type=jnp.float32)
    rowhot = (
        (a_idx[0][:, None] == jnp.arange(KR, dtype=jnp.int32)[None, :]) & live_a[:, None]
    ).astype(jnp.float32)
    result = jnp.einsum("sr,sxz->rxz", rowhot, prods, precision=lax.Precision.HIGHEST)
    return result.reshape(KR * side, KC * side)


def pick(take, moved, held):
    return jax.tree.map(lambda fresh, stale: jnp.where(take, fresh, stale), moved, held)


def local(a_blocks, a_index, a_count, b_blocks, b_index, b_count):
    row_id = lax.axis_index("row")
    col_id = lax.axis_index("col")
    grid_rows = lax.axis_size("row")
    grid_cols = lax.axis_size("col")
    left = (a_blocks[0, 0], a_index[0, 0], a_count[0])
    right = (b_blocks[:, 0, 0], b_index[:, 0, 0], b_count[:, 0, 0])
    section = 0
    while 1 << section < grid_rows:
        moved = jax.tree.map(
            lambda part, own: part.astype(own.dtype),
            passed_along(for_sending(left), "col", -(1 << section)),
            left,
        )
        left = pick(row_id >> section & 1 == 1, moved, left)
        section += 1
    b_amount = col_id % grid_rows
    section = 0
    while 1 << section < grid_rows:
        moved = jax.tree.map(
            lambda part, own: part.astype(own.dtype),
            passed_along(for_sending(right), "row", -(1 << section)),
            right,
        )
        right = pick(b_amount >> section & 1 == 1, moved, right)
        section += 1
    total = jnp.zeros((KR * BLOCK, KC * BLOCK), jnp.float32)
    for tick in range(TICKS):
        slot = (row_id + col_id + tick) % grid_cols // grid_rows
        b_blk = lax.dynamic_index_in_dim(right[0], slot, 0, keepdims=False)
        b_idx = lax.dynamic_index_in_dim(right[1], slot, 0, keepdims=False)
        b_cnt = lax.dynamic_index_in_dim(right[2], slot, 0, keepdims=True)
        total = total + panel_product(left[0], left[1], left[2], b_blk, b_idx, b_cnt)
        if tick + 1 < TICKS:
            left = jax.tree.map(
                lambda part, own: part.astype(own.dtype),
                passed_along(for_sending(left), "col", -1),
                left,
            )
            right = jax.tree.map(
                lambda part, own: part.astype(own.dtype),
                passed_along(for_sending(right), "row", -1),
                right,
            )
    return total.astype(jnp.bfloat16)


def solution(mesh):
    in_specs = (
        P("row", "col", None, None, None),
        P("row", "col", None, None),
        P("row", "col"),
        P(None, "row", "col", None, None, None),
        P(None, "row", "col", None, None),
        P(None, "row", "col"),
    )
    out_specs = P("row", "col")
    return jax.shard_map(local, mesh=mesh, in_specs=in_specs, out_specs=out_specs, check_vma=False)
```

profile of v0, /device:TPU:135, one launch (start us, length us, event | category | flops | bytes accessed | tf_op | source)
XLA Modules:
  0.0 657.9 jit_solution(11465401262239960913)
XLA Ops:
  5.5 19.8 %collective-permute-start.20 = (s32[1,2,6]{2,1,0:T(2,128)}, s32[1,2,6]{2,1,0:T(2,128)S(1)}, u32[]{:S(2)}, u32[]{:S(2)}) collective-permute-start(s32[1,2,6]{2,1,0:T(2,128)} %bitcast.140), channel_id=1, source_target_pairs={{32,0},{64,32},{96,64},{128,96},{160,128},{192,160},{224,192},{256... | collective-permute-start | bytes 152 | tf_op jit(solution)/shard_map/ppermute | solution.py:19
  35.8 7.6 %collective-permute-start.6 = (s32[1]{0:T(128)}, s32[1]{0:T(128)}, u32[]{:S(2)}, u32[]{:S(2)}) collective-permute-start(s32[1]{0:T(128)} %select_n.240), channel_id=1, source_target_pairs={{2,0},{3,1},{4,2},{5,3},{6,4},{7,5},{8,6},{9,7},{10,8},{11,9},{12,... | collective-permute-start | bytes 20 | tf_op jit(solution)/shard_map/ppermute | solution.py:19
  44.3 10.9 %collective-permute-start.26 = (s32[1]{0:T(128)}, s32[1]{0:T(128)}, u32[]{:S(2)}, u32[]{:S(2)}) collective-permute-start(s32[1]{0:T(128)} %select_n.281), channel_id=1, source_target_pairs={{64,0},{96,32},{128,64},{160,96},{192,128},{224,160},{256,192},{28... | collective-permute-start | bytes 20 | tf_op jit(solution)/shard_map/ppermute | solution.py:19
  59.9 6.0 collective-permute-start.7
  66.6 9.1 %collective-permute-start.27 = (s32[1]{0:T(128)}, s32[1]{0:T(128)}, u32[]{:S(2)}, u32[]{:S(2)}) collective-permute-start(s32[1]{0:T(128)} %select_n.282), channel_id=1, source_target_pairs={{128,0},{160,32},{192,64},{224,96},{256,128},{288,160},{320,192},{... | collective-permute-start | bytes 20 | tf_op jit(solution)/shard_map/ppermute | solution.py:19
  76.4 12.9 %collective-permute-done.27 = s32[1]{0:T(128)} collective-permute-done((s32[1]{0:T(128)}, s32[1]{0:T(128)}, u32[]{:S(2)}, u32[]{:S(2)}) %collective-permute-start.27) | collective-permute-done | bytes 36 | tf_op jit(solution)/shard_map/ppermute | solution.py:19
  89.4 6.7 %collective-permute-start.8 = (s32[1]{0:T(128)}, s32[1]{0:T(128)}, u32[]{:S(2)}, u32[]{:S(2)}) collective-permute-start(s32[1]{0:T(128)} %select_n.242), channel_id=1, source_target_pairs={{8,0},{9,1},{10,2},{11,3},{12,4},{13,5},{14,6},{15,7},{16,8},{17,9... | collective-permute-start | bytes 20 | tf_op jit(solution)/shard_map/ppermute | solution.py:19
  101.1 6.4 collective-permute-start.9
  115.3 18.6 %collective-permute-start.31 = (s32[1]{0:T(128)}, s32[1]{0:T(128)}, u32[]{:S(2)}, u32[]{:S(2)}) collective-permute-start(s32[1]{0:T(128)} %select_n.244), channel_id=1, source_target_pairs={{1,0},{2,1},{3,2},{4,3},{5,4},{6,5},{7,6},{8,7},{9,8},{10,9},{11,1... | collective-permute-start | bytes 20 | tf_op jit(solution)/shard_map/ppermute | solution.py:19
  138.9 15.4 %collective-permute-start.35 = (s32[1]{0:T(128)}, s32[1]{0:T(128)}, u32[]{:S(2)}, u32[]{:S(2)}) collective-permute-start(s32[1]{0:T(128)} %select_n.285), channel_id=1, source_target_pairs={{32,0},{64,32},{96,64},{128,96},{160,128},{192,160},{224,192},{256... | collective-permute-start | bytes 20 | tf_op jit(solution)/shard_map/ppermute | solution.py:19
  157.6 4.6 collective-permute-done.37
  166.6 9.4 %collective-permute-done.41 = s32[1]{0:T(128)} collective-permute-done((s32[1]{0:T(128)}, s32[1]{0:T(128)}, u32[]{:S(2)}, u32[]{:S(2)}) %collective-permute-start.41) | collective-permute-done | bytes 36 | tf_op jit(solution)/shard_map/ppermute | solution.py:19
  178.6 4.6 collective-permute-done.43
  183.2 5.1 collective-permute-start.47
  189.0 7.9 %collective-permute-done.47 = s32[1]{0:T(128)} collective-permute-done((s32[1]{0:T(128)}, s32[1]{0:T(128)}, u32[]{:S(2)}, u32[]{:S(2)}) %collective-permute-start.47) | collective-permute-done | bytes 36 | tf_op jit(solution)/shard_map/ppermute | solution.py:19
  198.3 18.3 %collective-permute-start.21 = (s32[1,2,6]{2,1,0:T(2,128)S(1)}, s32[1,2,6]{2,1,0:T(2,128)S(1)}, u32[]{:S(2)}, u32[]{:S(2)}) collective-permute-start(s32[1,2,6]{2,1,0:T(2,128)S(1)} %broadcast_select_fusion.10), channel_id=1, source_target_pairs={{64,0},{96,32},{128,64},{160,96},{192,128},{224,160},{256,192},{28... | collective-permute-start | bytes 152 | tf_op jit(solution)/shard_map/ppermute | solution.py:19
  217.3 16.0 %collective-permute-start.22 = (s32[1,2,6]{2,1,0:T(2,128)S(1)}, s32[1,2,6]{2,1,0:T(2,128)S(1)}, u32[]{:S(2)}, u32[]{:S(2)}) collective-permute-start(s32[1,2,6]{2,1,0:T(2,128)S(1)} %broadcast_select_fusion.11), channel_id=1, source_target_pairs={{128,0},{160,32},{192,64},{224,96},{256,128},{288,160},{320,192},{... | collective-permute-start | bytes 152 | tf_op jit(solution)/shard_map/ppermute | solution.py:19
  246.3 6.1 collective-permute-start.2
  256.2 9.8 %collective-permute-done.34 = s32[1,2,6]{2,1,0:T(2,128)S(1)} collective-permute-done((s32[1,2,6]{2,1,0:T(2,128)S(1)}, s32[1,2,6]{2,1,0:T(2,128)S(1)}, u32[]{:S(2)}, u32[]{:S(2)}) %collective-permute-start.34) | collective-permute-done | bytes 80 | tf_op jit(solution)/shard_map/ppermute | solution.py:19
  271.2 7.9 %collective-permute-start.40 = (s32[1,2,6]{2,1,0:T(2,128)S(1)}, s32[1,2,6]{2,1,0:T(2,128)S(1)}, u32[]{:S(2)}, u32[]{:S(2)}) collective-permute-start(s32[1,2,6]{2,1,0:T(2,128)S(1)} %collective-permute-done.34), channel_id=1, source_target_pairs={{32,0},{64,32},{96,64},{128,96},{160,128},{192,160},{224,192},{256... | collective-permute-start | bytes 152 | tf_op jit(solution)/shard_map/ppermute | solution.py:19
  279.1 5.7 collective-permute-done.40
  285.4 9.7 %collective-permute-start.46 = (s32[1,2,6]{2,1,0:T(2,128)S(1)}, s32[1,2,6]{2,1,0:T(2,128)S(1)}, u32[]{:S(2)}, u32[]{:S(2)}) collective-permute-start(s32[1,2,6]{2,1,0:T(2,128)S(1)} %collective-permute-done.40), channel_id=1, source_target_pairs={{32,0},{64,32},{96,64},{128,96},{160,128},{192,160},{224,192},{256... | collective-permute-start | bytes 152 | tf_op jit(solution)/shard_map/ppermute | solution.py:19
  295.1 17.8 %collective-permute-start.4 = (s32[2,12]{1,0:T(2,128)S(1)}, s32[2,12]{1,0:T(2,128)S(1)}, u32[]{:S(2)}, u32[]{:S(2)}) collective-permute-start(s32[2,12]{1,0:T(2,128)S(1)} %broadcast_select_fusion.18), channel_id=1, source_target_pairs={{16,0},{17,1},{18,2},{19,3},{20,4},{21,5},{22,6},{23,7},{24,8},{25... | collective-permute-start | bytes 296 | tf_op jit(solution)/shard_map/ppermute | solution.py:19
  331.3 14.0 %collective-permute-start.16 = (bf16[1,6,128,128]{3,1,2,0:T(8,128)(2,1)S(1)}, bf16[1,6,128,128]{3,1,2,0:T(8,128)(2,1)S(1)}, u32[]{:S(2)}, u32[]{:S(2)}) collective-permute-start(bf16[1,6,128,128]{3,1,2,0:T(8,128)(2,1)S(1)} %broadcast_select_fusion.5), channel_id=1, source_target_pairs={{64,0},{96,32},{128,64},{160,96},{192,128},{224,160},{256,192},{28... | collective-permute-start | bytes 589832 | tf_op jit(solution)/shard_map/ppermute | solution.py:19
  345.4 11.3 %collective-permute-done.16 = bf16[1,6,128,128]{3,1,2,0:T(8,128)(2,1)S(1)} collective-permute-done((bf16[1,6,128,128]{3,1,2,0:T(8,128)(2,1)S(1)}, bf16[1,6,128,128]{3,1,2,0:T(8,128)(2,1)S(1)}, u32[]{:S(2)}, u32[]{:S(2)}) %collective-permute-start.16) | collective-permute-done | bytes 196640 | tf_op jit(solution)/shard_map/ppermute | solution.py:19
  356.7 30.2 %collective-permute-start.17 = (bf16[1,6,128,128]{3,1,2,0:T(8,128)(2,1)S(1)}, bf16[1,6,128,128]{3,1,2,0:T(8,128)(2,1)S(1)}, u32[]{:S(2)}, u32[]{:S(2)}) collective-permute-start(bf16[1,6,128,128]{3,1,2,0:T(8,128)(2,1)S(1)} %broadcast_select_fusion.6), channel_id=1, source_target_pairs={{128,0},{160,32},{192,64},{224,96},{256,128},{288,160},{320,192},{... | collective-permute-start | bytes 589832 | tf_op jit(solution)/shard_map/ppermute | solution.py:19
  392.2 56.8 %collective-permute-start.18 = (bf16[1,6,128,128]{3,1,2,0:T(8,128)(2,1)S(1)}, bf16[1,6,128,128]{3,1,2,0:T(8,128)(2,1)S(1)}, u32[]{:S(2)}, u32[]{:S(2)}) collective-permute-start(bf16[1,6,128,128]{3,1,2,0:T(8,128)(2,1)S(1)} %broadcast_select_fusion.7), channel_id=1, source_target_pairs={{256,0},{288,32},{320,64},{352,96},{384,128},{416,160},{448,192},{... | collective-permute-start | bytes 589832 | tf_op jit(solution)/shard_map/ppermute | solution.py:19
  471.8 110.2 %collective-permute-done.33 = bf16[1,6,128,128]{3,1,2,0:T(8,128)(2,1)} collective-permute-done((bf16[1,6,128,128]{3,1,2,0:T(8,128)(2,1)S(1)}, bf16[1,6,128,128]{3,1,2,0:T(8,128)(2,1)}, u32[]{:S(2)}, u32[]{:S(2)}) %collective-permute-start.33) | collective-permute-done | bytes 196640 | tf_op jit(solution)/shard_map/ppermute | solution.py:19
  590.5 8.1 %collective-permute-done.39 = bf16[1,6,128,128]{3,1,2,0:T(8,128)(2,1)S(1)} collective-permute-done((bf16[1,6,128,128]{3,1,2,0:T(8,128)(2,1)}, bf16[1,6,128,128]{3,1,2,0:T(8,128)(2,1)S(1)}, u32[]{:S(2)}, u32[]{:S(2)}) %collective-permute-start.39) | collective-permute-done | bytes 196640 | tf_op jit(solution)/shard_map/ppermute | solution.py:19
  606.1 12.5 %collective-permute-done.45 = bf16[1,6,128,128]{3,1,2,0:T(8,128)(2,1)S(1)} collective-permute-done((bf16[1,6,128,128]{3,1,2,0:T(8,128)(2,1)S(1)}, bf16[1,6,128,128]{3,1,2,0:T(8,128)(2,1)S(1)}, u32[]{:S(2)}, u32[]{:S(2)}) %collective-permute-start.45) | collective-permute-done | bytes 196640 | tf_op jit(solution)/shard_map/ppermute | solution.py:19
  630.4 8.1 %collective-permute-done.38 = bf16[12,128,128]{2,1,0:T(8,128)(2,1)S(1)} collective-permute-done((bf16[12,128,128]{2,1,0:T(8,128)(2,1)S(1)}, bf16[12,128,128]{2,1,0:T(8,128)(2,1)S(1)}, u32[]{:S(2)}, u32[]{:S(2)}) %collective-permute-start.38) | collective-permute-done | bytes 393248 | tf_op jit(solution)/shard_map/ppermute | solution.py:19
  644.3 4.8 collective-permute-done.44
  (158 shorter events, 156.4 us)
Async XLA Ops:
  0.0 33.0 %collective-permute-start.5 = (s32[1]{0:T(128)}, s32[1]{0:T(128)}, u32[]{:S(2)}, u32[]{:S(2)}) collective-permute-start(s32[1]{0:T(128)} %bitcast.7), channel_id=1, source_target_pairs={{1,0},{2,1},{3,2},{4,3},{5,4},{6,5},{7,6},{8,7},{9,8},{10,9},{11,1... | collective-permute-start | bytes 20 | tf_op jit(solution)/shard_map/ppermute | solution.py:19
  2.6 33.2 %collective-permute-start.25 = (s32[1]{0:T(128)}, s32[1]{0:T(128)}, u32[]{:S(2)}, u32[]{:S(2)}) collective-permute-start(s32[1]{0:T(128)} %bitcast.23), channel_id=1, source_target_pairs={{32,0},{64,32},{96,64},{128,96},{160,128},{192,160},{224,192},{256... | collective-permute-start | bytes 20 | tf_op jit(solution)/shard_map/ppermute | solution.py:19
  5.5 192.1 %collective-permute-start.20 = (s32[1,2,6]{2,1,0:T(2,128)}, s32[1,2,6]{2,1,0:T(2,128)S(1)}, u32[]{:S(2)}, u32[]{:S(2)}) collective-permute-start(s32[1,2,6]{2,1,0:T(2,128)} %bitcast.140), channel_id=1, source_target_pairs={{32,0},{64,32},{96,64},{128,96},{160,128},{192,160},{224,192},{256... | collective-permute-start | bytes 152 | tf_op jit(solution)/shard_map/ppermute | solution.py:19
  25.3 208.0 %collective-permute-start = (s32[2,12]{1,0:T(2,128)}, s32[2,12]{1,0:T(2,128)S(1)}, u32[]{:S(2)}, u32[]{:S(2)}) collective-permute-start(s32[2,12]{1,0:T(2,128)} %bitcast.141), channel_id=1, source_target_pairs={{1,0},{2,1},{3,2},{4,3},{5,4},{6,5},{7,6},{8,7},{9,8},{10,9},{11,1... | collective-permute-start | bytes 296 | tf_op jit(solution)/shard_map/ppermute | solution.py:19
  28.5 301.7 %collective-permute-start.15 = (bf16[1,6,128,128]{3,1,2,0:T(8,128)(2,1)S(1)}, bf16[1,6,128,128]{3,1,2,0:T(8,128)(2,1)S(1)}, u32[]{:S(2)}, u32[]{:S(2)}) collective-permute-start(bf16[1,6,128,128]{3,1,2,0:T(8,128)(2,1)S(1)} %bitcast.139), channel_id=1, source_target_pairs={{32,0},{64,32},{96,64},{128,96},{160,128},{192,160},{224,192},{256... | collective-permute-start | bytes 589832 | tf_op jit(solution)/shard_map/ppermute | solution.py:19
  33.0 353.9 %collective-permute-start.10 = (bf16[12,128,128]{2,1,0:T(8,128)(2,1)}, bf16[12,128,128]{2,1,0:T(8,128)(2,1)S(1)}, u32[]{:S(2)}, u32[]{:S(2)}) collective-permute-start(bf16[12,128,128]{2,1,0:T(8,128)(2,1)} %bitcast.138), channel_id=1, source_target_pairs={{1,0},{2,1},{3,2},{4,3},{5,4},{6,5},{7,6},{8,7},{9,8},{10,9},{11,1... | collective-permute-start | bytes 1179656 | tf_op jit(solution)/shard_map/ppermute | solution.py:19
  44.3 15.6 %collective-permute-start.26 = (s32[1]{0:T(128)}, s32[1]{0:T(128)}, u32[]{:S(2)}, u32[]{:S(2)}) collective-permute-start(s32[1]{0:T(128)} %select_n.281), channel_id=1, source_target_pairs={{64,0},{96,32},{128,64},{160,96},{192,128},{224,160},{256,192},{28... | collective-permute-start | bytes 20 | tf_op jit(solution)/shard_map/ppermute | solution.py:19
  66.6 22.7 %collective-permute-start.27 = (s32[1]{0:T(128)}, s32[1]{0:T(128)}, u32[]{:S(2)}, u32[]{:S(2)}) collective-permute-start(s32[1]{0:T(128)} %select_n.282), channel_id=1, source_target_pairs={{128,0},{160,32},{192,64},{224,96},{256,128},{288,160},{320,192},{... | collective-permute-start | bytes 20 | tf_op jit(solution)/shard_map/ppermute | solution.py:19
  115.3 23.6 %collective-permute-start.31 = (s32[1]{0:T(128)}, s32[1]{0:T(128)}, u32[]{:S(2)}, u32[]{:S(2)}) collective-permute-start(s32[1]{0:T(128)} %select_n.244), channel_id=1, source_target_pairs={{1,0},{2,1},{3,2},{4,3},{5,4},{6,5},{7,6},{8,7},{9,8},{10,9},{11,1... | collective-permute-start | bytes 20 | tf_op jit(solution)/shard_map/ppermute | solution.py:19
  138.9 16.1 %collective-permute-start.35 = (s32[1]{0:T(128)}, s32[1]{0:T(128)}, u32[]{:S(2)}, u32[]{:S(2)}) collective-permute-start(s32[1]{0:T(128)} %select_n.285), channel_id=1, source_target_pairs={{32,0},{64,32},{96,64},{128,96},{160,128},{192,160},{224,192},{256... | collective-permute-start | bytes 20 | tf_op jit(solution)/shard_map/ppermute | solution.py:19
  162.2 13.7 %collective-permute-start.41 = (s32[1]{0:T(128)}, s32[1]{0:T(128)}, u32[]{:S(2)}, u32[]{:S(2)}) collective-permute-start(s32[1]{0:T(128)} %collective-permute-done.35), channel_id=1, source_target_pairs={{32,0},{64,32},{96,64},{128,96},{160,128},{192,160},{224,192},{256... | collective-permute-start | bytes 20 | tf_op jit(solution)/shard_map/ppermute | solution.py:19
  183.2 13.7 %collective-permute-start.47 = (s32[1]{0:T(128)}, s32[1]{0:T(128)}, u32[]{:S(2)}, u32[]{:S(2)}) collective-permute-start(s32[1]{0:T(128)} %collective-permute-done.41), channel_id=1, source_target_pairs={{32,0},{64,32},{96,64},{128,96},{160,128},{192,160},{224,192},{256... | collective-permute-start | bytes 20 | tf_op jit(solution)/shard_map/ppermute | solution.py:19
  198.3 19.0 %collective-permute-start.21 = (s32[1,2,6]{2,1,0:T(2,128)S(1)}, s32[1,2,6]{2,1,0:T(2,128)S(1)}, u32[]{:S(2)}, u32[]{:S(2)}) collective-permute-start(s32[1,2,6]{2,1,0:T(2,128)S(1)} %broadcast_select_fusion.10), channel_id=1, source_target_pairs={{64,0},{96,32},{128,64},{160,96},{192,128},{224,160},{256,192},{28... | collective-permute-start | bytes 152 | tf_op jit(solution)/shard_map/ppermute | solution.py:19
  217.3 22.7 %collective-permute-start.22 = (s32[1,2,6]{2,1,0:T(2,128)S(1)}, s32[1,2,6]{2,1,0:T(2,128)S(1)}, u32[]{:S(2)}, u32[]{:S(2)}) collective-permute-start(s32[1,2,6]{2,1,0:T(2,128)S(1)} %broadcast_select_fusion.11), channel_id=1, source_target_pairs={{128,0},{160,32},{192,64},{224,96},{256,128},{288,160},{320,192},{... | collective-permute-start | bytes 152 | tf_op jit(solution)/shard_map/ppermute | solution.py:19
  246.3 20.3 %collective-permute-start.2 = (s32[2,12]{1,0:T(2,128)S(1)}, s32[2,12]{1,0:T(2,128)S(1)}, u32[]{:S(2)}, u32[]{:S(2)}) collective-permute-start(s32[2,12]{1,0:T(2,128)S(1)} %broadcast_select_fusion.16), channel_id=1, source_target_pairs={{4,0},{5,1},{6,2},{7,3},{8,4},{9,5},{10,6},{11,7},{12,8},{13,9},{1... | collective-permute-start | bytes 296 | tf_op jit(solution)/shard_map/ppermute | solution.py:19
  252.4 13.6 %collective-permute-start.34 = (s32[1,2,6]{2,1,0:T(2,128)S(1)}, s32[1,2,6]{2,1,0:T(2,128)S(1)}, u32[]{:S(2)}, u32[]{:S(2)}) collective-permute-start(s32[1,2,6]{2,1,0:T(2,128)S(1)} %broadcast_select_fusion.14), channel_id=1, source_target_pairs={{32,0},{64,32},{96,64},{128,96},{160,128},{192,160},{224,192},{256... | collective-permute-start | bytes 152 | tf_op jit(solution)/shard_map/ppermute | solution.py:19
  266.6 28.5 %collective-permute-start.3 = (s32[2,12]{1,0:T(2,128)S(1)}, s32[2,12]{1,0:T(2,128)S(1)}, u32[]{:S(2)}, u32[]{:S(2)}) collective-permute-start(s32[2,12]{1,0:T(2,128)S(1)} %broadcast_select_fusion.17), channel_id=1, source_target_pairs={{8,0},{9,1},{10,2},{11,3},{12,4},{13,5},{14,6},{15,7},{16,8},{17,9... | collective-permute-start | bytes 296 | tf_op jit(solution)/shard_map/ppermute | solution.py:19
  271.2 13.6 %collective-permute-start.40 = (s32[1,2,6]{2,1,0:T(2,128)S(1)}, s32[1,2,6]{2,1,0:T(2,128)S(1)}, u32[]{:S(2)}, u32[]{:S(2)}) collective-permute-start(s32[1,2,6]{2,1,0:T(2,128)S(1)} %collective-permute-done.34), channel_id=1, source_target_pairs={{32,0},{64,32},{96,64},{128,96},{160,128},{192,160},{224,192},{256... | collective-permute-start | bytes 152 | tf_op jit(solution)/shard_map/ppermute | solution.py:19
  285.4 27.6 %collective-permute-start.46 = (s32[1,2,6]{2,1,0:T(2,128)S(1)}, s32[1,2,6]{2,1,0:T(2,128)S(1)}, u32[]{:S(2)}, u32[]{:S(2)}) collective-permute-start(s32[1,2,6]{2,1,0:T(2,128)S(1)} %collective-permute-done.40), channel_id=1, source_target_pairs={{32,0},{64,32},{96,64},{128,96},{160,128},{192,160},{224,192},{256... | collective-permute-start | bytes 152 | tf_op jit(solution)/shard_map/ppermute | solution.py:19
  295.1 18.8 %collective-permute-start.4 = (s32[2,12]{1,0:T(2,128)S(1)}, s32[2,12]{1,0:T(2,128)S(1)}, u32[]{:S(2)}, u32[]{:S(2)}) collective-permute-start(s32[2,12]{1,0:T(2,128)S(1)} %broadcast_select_fusion.18), channel_id=1, source_target_pairs={{16,0},{17,1},{18,2},{19,3},{20,4},{21,5},{22,6},{23,7},{24,8},{25... | collective-permute-start | bytes 296 | tf_op jit(solution)/shard_map/ppermute | solution.py:19
  327.9 61.1 %collective-permute-start.42 = (s32[2,12]{1,0:T(2,128)S(1)}, s32[2,12]{1,0:T(2,128)S(1)}, u32[]{:S(2)}, u32[]{:S(2)}) collective-permute-start(s32[2,12]{1,0:T(2,128)S(1)} %collective-permute-done.36), channel_id=1, source_target_pairs={{1,0},{2,1},{3,2},{4,3},{5,4},{6,5},{7,6},{8,7},{9,8},{10,9},{11,1... | collective-permute-start | bytes 296 | tf_op jit(solution)/shard_map/ppermute | solution.py:19
  331.3 25.4 %collective-permute-start.16 = (bf16[1,6,128,128]{3,1,2,0:T(8,128)(2,1)S(1)}, bf16[1,6,128,128]{3,1,2,0:T(8,128)(2,1)S(1)}, u32[]{:S(2)}, u32[]{:S(2)}) collective-permute-start(bf16[1,6,128,128]{3,1,2,0:T(8,128)(2,1)S(1)} %broadcast_select_fusion.5), channel_id=1, source_target_pairs={{64,0},{96,32},{128,64},{160,96},{192,128},{224,160},{256,192},{28... | collective-permute-start | bytes 589832 | tf_op jit(solution)/shard_map/ppermute | solution.py:19
  356.7 35.4 %collective-permute-start.17 = (bf16[1,6,128,128]{3,1,2,0:T(8,128)(2,1)S(1)}, bf16[1,6,128,128]{3,1,2,0:T(8,128)(2,1)S(1)}, u32[]{:S(2)}, u32[]{:S(2)}) collective-permute-start(bf16[1,6,128,128]{3,1,2,0:T(8,128)(2,1)S(1)} %broadcast_select_fusion.6), channel_id=1, source_target_pairs={{128,0},{160,32},{192,64},{224,96},{256,128},{288,160},{320,192},{... | collective-permute-start | bytes 589832 | tf_op jit(solution)/shard_map/ppermute | solution.py:19
  387.0 61.9 %collective-permute-start.11 = (bf16[12,128,128]{2,1,0:T(8,128)(2,1)S(1)}, bf16[12,128,128]{2,1,0:T(8,128)(2,1)S(1)}, u32[]{:S(2)}, u32[]{:S(2)}) collective-permute-start(bf16[12,128,128]{2,1,0:T(8,128)(2,1)S(1)} %broadcast_select_fusion), channel_id=1, source_target_pairs={{2,0},{3,1},{4,2},{5,3},{6,4},{7,5},{8,6},{9,7},{10,8},{11,9},{12,... | collective-permute-start | bytes 1179656 | tf_op jit(solution)/shard_map/ppermute | solution.py:19
  392.2 61.8 %collective-permute-start.18 = (bf16[1,6,128,128]{3,1,2,0:T(8,128)(2,1)S(1)}, bf16[1,6,128,128]{3,1,2,0:T(8,128)(2,1)S(1)}, u32[]{:S(2)}, u32[]{:S(2)}) collective-permute-start(bf16[1,6,128,128]{3,1,2,0:T(8,128)(2,1)S(1)} %broadcast_select_fusion.7), channel_id=1, source_target_pairs={{256,0},{288,32},{320,64},{352,96},{384,128},{416,160},{448,192},{... | collective-permute-start | bytes 589832 | tf_op jit(solution)/shard_map/ppermute | solution.py:19
  460.6 123.3 %collective-permute-start.13 = (bf16[12,128,128]{2,1,0:T(8,128)(2,1)S(1)}, bf16[12,128,128]{2,1,0:T(8,128)(2,1)S(1)}, u32[]{:S(2)}, u32[]{:S(2)}) collective-permute-start(bf16[12,128,128]{2,1,0:T(8,128)(2,1)S(1)} %broadcast_select_fusion.2), channel_id=1, source_target_pairs={{8,0},{9,1},{10,2},{11,3},{12,4},{13,5},{14,6},{15,7},{16,8},{17,9... | collective-permute-start | bytes 1179656 | tf_op jit(solution)/shard_map/ppermute | solution.py:19
  464.4 117.6 %collective-permute-start.33 = (bf16[1,6,128,128]{3,1,2,0:T(8,128)(2,1)S(1)}, bf16[1,6,128,128]{3,1,2,0:T(8,128)(2,1)}, u32[]{:S(2)}, u32[]{:S(2)}) collective-permute-start(bf16[1,6,128,128]{3,1,2,0:T(8,128)(2,1)S(1)} %broadcast_select_fusion.9), channel_id=1, source_target_pairs={{32,0},{64,32},{96,64},{128,96},{160,128},{192,160},{224,192},{256... | collective-permute-start | bytes 589832 | tf_op jit(solution)/shard_map/ppermute | solution.py:19
  582.0 16.6 %collective-permute-start.39 = (bf16[1,6,128,128]{3,1,2,0:T(8,128)(2,1)}, bf16[1,6,128,128]{3,1,2,0:T(8,128)(2,1)S(1)}, u32[]{:S(2)}, u32[]{:S(2)}) collective-permute-start(bf16[1,6,128,128]{3,1,2,0:T(8,128)(2,1)} %collective-permute-done.33), channel_id=1, source_target_pairs={{32,0},{64,32},{96,64},{128,96},{160,128},{192,160},{224,192},{256... | collective-permute-start | bytes 589832 | tf_op jit(solution)/shard_map/ppermute | solution.py:19
  584.0 20.1 %collective-permute-start.14 = (bf16[12,128,128]{2,1,0:T(8,128)(2,1)S(1)}, bf16[12,128,128]{2,1,0:T(8,128)(2,1)S(1)}, u32[]{:S(2)}, u32[]{:S(2)}) collective-permute-start(bf16[12,128,128]{2,1,0:T(8,128)(2,1)S(1)} %broadcast_select_fusion.3), channel_id=1, source_target_pairs={{16,0},{17,1},{18,2},{19,3},{20,4},{21,5},{22,6},{23,7},{24,8},{25... | collective-permute-start | bytes 1179656 | tf_op jit(solution)/shard_map/ppermute | solution.py:19
  602.2 16.4 %collective-permute-start.45 = (bf16[1,6,128,128]{3,1,2,0:T(8,128)(2,1)S(1)}, bf16[1,6,128,128]{3,1,2,0:T(8,128)(2,1)S(1)}, u32[]{:S(2)}, u32[]{:S(2)}) collective-permute-start(bf16[1,6,128,128]{3,1,2,0:T(8,128)(2,1)S(1)} %collective-permute-done.39), channel_id=1, source_target_pairs={{32,0},{64,32},{96,64},{128,96},{160,128},{192,160},{224,192},{256... | collective-permute-start | bytes 589832 | tf_op jit(solution)/shard_map/ppermute | solution.py:19
  604.2 20.1 %collective-permute-start.32 = (bf16[12,128,128]{2,1,0:T(8,128)(2,1)S(1)}, bf16[12,128,128]{2,1,0:T(8,128)(2,1)S(1)}, u32[]{:S(2)}, u32[]{:S(2)}) collective-permute-start(bf16[12,128,128]{2,1,0:T(8,128)(2,1)S(1)} %broadcast_select_fusion.4), channel_id=1, source_target_pairs={{1,0},{2,1},{3,2},{4,3},{5,4},{6,5},{7,6},{8,7},{9,8},{10,9},{11,1... | collective-permute-start | bytes 1179656 | tf_op jit(solution)/shard_map/ppermute | solution.py:19
  624.3 14.1 %collective-permute-start.38 = (bf16[12,128,128]{2,1,0:T(8,128)(2,1)S(1)}, bf16[12,128,128]{2,1,0:T(8,128)(2,1)S(1)}, u32[]{:S(2)}, u32[]{:S(2)}) collective-permute-start(bf16[12,128,128]{2,1,0:T(8,128)(2,1)S(1)} %collective-permute-done.32), channel_id=1, source_target_pairs={{1,0},{2,1},{3,2},{4,3},{5,4},{6,5},{7,6},{8,7},{9,8},{10,9},{11,1... | collective-permute-start | bytes 1179656 | tf_op jit(solution)/shard_map/ppermute | solution.py:19
  (32 other events, 1350.2 us)
where the time goes:
time: 660 us; the launch traced here: 658 us
  starting transfers between devices  355 us (54%)
  waiting for transfers between devices  248 us (38%)
  matrix products  21.3 us (3%)
  local copies, waits for them, and re-layouts  15.8 us (2%)
  between operations  8.91 us (1%)
  other arithmetic  8.74 us (1%)
    ppermute x48, starting transfers between devices, passed_along(): return lax.ppermute(block, axis, route)  355 us
    ppermute x48, waiting for transfers between devices, passed_along(): return lax.ppermute(block, axis, route)  248 us
    dot_general x4, matrix products, panel_product(): jnp.einsum('sr,sxz->rxz', rowhot, prods, precision=lax.Precision.HIGHEST)  13.3 us
  transfers between devices with their start and end apart: 48, of which 28 were waited for; matrix products, arithmetic and copies ran while one was open for 6% of the time, Pallas kernels for 0%

commit v1 on v0

v1 whole, which is shorter than its diff:
```python
import jax
import jax.numpy as jnp
import numpy as np
from jax import lax
from jax.experimental import pallas as pl
from jax.experimental.pallas import tpu as pltpu
from jax.sharding import PartitionSpec as P

BLOCK = 128
KR = 8
KC = 4
TICKS = 4
SA = 12
SB = 6
GRID = 32
CHIPS = GRID // 2
TAG = 16
AXES = ("row", "col")

ROLES = {
    (0, 0): {"first": "F", "near": "O", "relay": "H"},
    (0, 1): {"first": "O", "near": "H", "relay": "F"},
    (0, 2): {"first": "F", "near": "H", "relay": "O"},
    (0, 3): {"first": "O", "near": "F", "last": "H"},
    (1, 0): {"first": "F", "near": "H", "relay": "O"},
    (1, 1): {"first": "O", "near": "H", "relay": "F"},
    (1, 2): {"first": "F", "near": "O", "relay": "H"},
    (1, 3): {"first": "O", "near": "F", "last": "H"},
}
MOVES = ("first", "near", "last", "relay")
SWAPS = ("first", "near", "relay")


def offset_of(role, p):
    return {"F": 1, "O": 2 * p, "H": 2 - 2 * p}[role]


def tick_of(role, p, c):
    if role == "F":
        return 2 - p
    if role == "O":
        return 3 * p
    return (3 - 3 * p) if c != p else -1


def tick_of_swap(role, p, c):
    if role == "F":
        return 3 - 2 * c - p
    return 1 + p if c == p else -1


def plan():
    pairs = {name: [] for name in MOVES}
    swaps = {name: [] for name in SWAPS}
    ticks = np.full((2, 2, 4, 8), -1, np.int32)
    for j in range(GRID):
        shift, p = j // 2, j % 2
        d = shift % 4
        roles = ROLES[p, d]
        for c in range(2):
            for at, name in enumerate(MOVES):
                if name in roles:
                    ticks[p, c, d, at] = tick_of(roles[name], p, c)
            for at, name in enumerate(SWAPS):
                if roles.get(name, "H") != "H":
                    ticks[p, c, d, len(MOVES) + at] = tick_of_swap(roles[name], p, c)
            for chip in range(CHIPS):
                here = (2 * chip + c) * GRID + j
                for at, name in enumerate(MOVES):
                    if ticks[p, c, d, at] < 0:
                        continue
                    role = roles[name]
                    core = 1 - c if role == "H" else c
                    if name == "relay":
                        source = chip + offset_of(role, p) - offset_of(roles["first"], p)
                    else:
                        source = chip + shift + offset_of(role, p)
                    source = (2 * (source % CHIPS) + core) * GRID + j
                    pairs[name].append((source, here))
                for at, name in enumerate(SWAPS):
                    if ticks[p, c, d, len(MOVES) + at] >= 0:
                        swaps[name].append(((2 * chip + 1 - c) * GRID + j, here))
    return pairs, swaps, ticks


def left_plan():
    skew, before, after, after2 = [], [], [], []
    wrap, wrap2 = [], []
    for i in range(GRID):
        at = lambda col: i * GRID + col % GRID
        for j in range(GRID):
            skew.append((at(i + j + 1), at(j)))
            if j > 0:
                before.append((at(j - 1), at(j)))
            if j < GRID - 1:
                after.append((at(j + 1), at(j)))
            if j < GRID - 2:
                after2.append((at(j + 1), at(j)))
        wrap += [(at(i), at(0)), (at(i + 1), at(GRID - 1))]
        wrap2 += [(at(i + 1), at(GRID - 2)), (at(i + 2), at(GRID - 1))]
    return skew, before, after, after2, wrap, wrap2


def tagged(blocks, index, count, empty):
    slots = blocks.shape[0]
    live = jnp.arange(slots, dtype=jnp.int32) < count
    first = index[0]
    second = index[1]
    if empty == 65:
        first = jnp.where(live, first, empty)
    else:
        second = jnp.where(live, second, empty)
    tag = jnp.stack([first, second]).astype(jnp.bfloat16)
    tag = jnp.pad(tag, ((0, TAG - 2), (0, BLOCK - slots)))
    return jnp.concatenate([blocks.reshape(slots * BLOCK, BLOCK), tag])


def kernel(tick_ref, *refs):
    a_refs = refs[:TICKS]
    n_b = len(MOVES) + len(SWAPS)
    b_refs = refs[TICKS : TICKS + n_b]
    out_ref, acc, tags, scal, sem = refs[TICKS + n_b :]
    for t, ref in enumerate(a_refs):
        tags[t] = ref[SA * BLOCK : SA * BLOCK + TAG, :].astype(jnp.float32)[:8].astype(jnp.int32)
    for b, ref in enumerate(b_refs):
        tags[TICKS + b] = ref[SB * BLOCK : SB * BLOCK + TAG, :].astype(jnp.float32)[:8].astype(jnp.int32)
    copy = pltpu.make_async_copy(tags, scal, sem)
    copy.start()
    acc[...] = jnp.zeros_like(acc)
    copy.wait()

    def multiply(t, b):
        a_ref, b_ref = a_refs[t], b_refs[b]

        def slot(u, carry):
            row = scal[TICKS + b, 0, u]
            hits = jnp.int32(0)
            for s in range(SA):
                hits = hits | jnp.where(scal[t, 1, s] == row, 1 << s, 0)

            @pl.when(hits != 0)
            def _():
                right = b_ref[pl.ds(pl.multiple_of(u * BLOCK, BLOCK), BLOCK), :]
                column = scal[TICKS + b, 1, u]

                def product(s, carry):
                    @pl.when((hits >> s) & 1 == 1)
                    def _():
                        left = a_ref[pl.ds(pl.multiple_of(s * BLOCK, BLOCK), BLOCK), :]
                        place = scal[t, 0, s] * KC + column
                        acc[place] += jnp.dot(left, right, preferred_element_type=jnp.float32)

                    return carry

                lax.fori_loop(0, SA, product, 0)

            return carry

        lax.fori_loop(0, SB, slot, 0)

    for b in range(n_b):
        for t in range(TICKS):
            pl.when(tick_ref[b] == t)(lambda t=t, b=b: multiply(t, b))
    for r in range(KR):
        for c in range(KC):
            out_ref[r * BLOCK : (r + 1) * BLOCK, c * BLOCK : (c + 1) * BLOCK] = acc[r * KC + c].astype(jnp.bfloat16)


def multiply_all(ticks, lefts, rights):
    n = len(lefts) + len(rights)
    return pl.pallas_call(
        kernel,
        out_shape=jax.ShapeDtypeStruct((KR * BLOCK, KC * BLOCK), jnp.bfloat16),
        in_specs=[pl.BlockSpec(memory_space=pltpu.SMEM)] + [pl.BlockSpec(memory_space=pltpu.VMEM)] * n,
        out_specs=pl.BlockSpec(memory_space=pltpu.VMEM),
        scratch_shapes=[
            pltpu.VMEM((KR * KC, BLOCK, BLOCK), jnp.float32),
            pltpu.VMEM((n, 8, BLOCK), jnp.int32),
            pltpu.SMEM((n, 8, BLOCK), jnp.int32),
            pltpu.SemaphoreType.DMA,
        ],
        compiler_params=pltpu.CompilerParams(vmem_limit_bytes=24 * 1024 * 1024),
    )(ticks, *lefts, *rights)


def local(a_blocks, a_index, a_count, b_blocks, b_index, b_count):
    row_id = lax.axis_index("row")
    col_id = lax.axis_index("col")
    pairs, swap_pairs, ticks = plan()
    ticks = jnp.asarray(ticks)[col_id % 2, row_id % 2, col_id // 2 % 4]
    left = tagged(a_blocks[0, 0], a_index[0, 0], a_count[0, 0], 64)
    right = tagged(b_blocks[0, 0, 0], b_index[0, 0, 0], b_count[0, 0, 0], 65)

    def send(value, route):
        return lax.ppermute(value, AXES, route)

    skew, before, after, after2, wrap, wrap2 = left_plan()
    moved = {"first": send(right, pairs["first"])}
    left1 = send(left, skew)
    moved["near"] = send(right, pairs["near"])
    moved["last"] = send(right, pairs["last"])
    wrapped = send(left, wrap)
    wrapped2 = send(left, wrap2)
    moved["relay"] = send(moved["first"], pairs["relay"])
    left2 = send(left1, after)
    left0 = send(left1, before)
    left2 = jnp.where(col_id == GRID - 1, wrapped, left2)
    left0 = jnp.where(col_id == 0, wrapped, left0)
    left3 = send(left2, after2)
    left3 = jnp.where(col_id >= GRID - 2, wrapped2, left3)
    swapped = [send(moved[name], swap_pairs[name]) for name in SWAPS]
    return multiply_all(ticks, (left0, left1, left2, left3), [moved[name] for name in MOVES] + swapped)


def solution(mesh):
    in_specs = (
        P("row", "col", None, None, None),
        P("row", "col", None, None),
        P("row", "col"),
        P(None, "row", "col", None, None, None),
        P(None, "row", "col", None, None),
        P(None, "row", "col"),
    )
    out_specs = P("row", "col")
    return jax.shard_map(local, mesh=mesh, in_specs=in_specs, out_specs=out_specs, check_vma=False)
```

time: 660 us -> 132 us (0.20)
  the two profiles are of different devices: /device:TPU:135 before, /device:TPU:23 now
where the time goes in v1:
time: 132 us
  starting transfers between devices  71.9 us (54%)
  waiting for transfers between devices  50.3 us (38%)
  Pallas kernels  4.99 us (4%)
  other arithmetic  1.94 us (1%)
  between operations  1.64 us (1%)
    ppermute x13, starting transfers between devices, send(): return lax.ppermute(value, AXES, route)  71.9 us
    ppermute x13, waiting for transfers between devices, send(): return lax.ppermute(value, AXES, route)  50.3 us
    pallas_call x1, Pallas kernels, multiply_all(): pl.pallas_call(kernel, out_shape=jax.ShapeDtypeStruct((KR * BLOCK, KC * B...  4.99 us
  transfers between devices with their start and end apart: 13, of which 5 were waited for; matrix products, arithmetic and copies ran while one was open for 1% of the time, Pallas kernels for 0%

profile of v1, /device:TPU:23, one launch (start us, length us, event | category | flops | bytes accessed | tf_op | source)
XLA Modules:
  0.0 131.5 jit_solution(4375455894923856002)
XLA Ops:
  0.7 0.0 copy-done.1
  0.7 0.0 copy-start
  0.7 1.1 pad_maximum_fusion
  1.8 0.0 copy-start.2
  1.8 9.7 %collective-permute-start.1 = (bf16[1552,128]{1,0:T(8,128)(2,1)S(1)}, bf16[1552,128]{1,0:T(8,128)(2,1)S(1)}, u32[]{:S(2)}, u32[]{:S(2)}) collective-permute-start(bf16[1552,128]{1,0:T(8,128)(2,1)S(1)} %pad_maximum_fusion), channel_id=1, source_target_pairs={{1,0},{2,1},{3,2},{4,3},{5,4},{6,5},{7,6},{8,7},{9,8},{10,9},{11,1... | collective-permute-start | bytes 1191944 | tf_op jit(solution)/shard_map/ppermute | solution.py:195
  11.5 0.7 collective-permute-start
  12.2 0.7 collective-permute-start.4
  13.6 25.3 %collective-permute-done.1.refs_1_ = bf16[1552,128]{1,0:T(8,128)(2,1)S(1)} collective-permute-done((bf16[1552,128]{1,0:T(8,128)(2,1)S(1)}, bf16[1552,128]{1,0:T(8,128)(2,1)S(1)}, u32[]{:S(2)}, u32[]{:S(2)}) %collective-permute-start.1) | collective-permute-done | bytes 397344 | tf_op jit(solution)/shard_map/ppermute | solution.py:195
  38.8 3.5 %collective-permute-start.2 = (bf16[1552,128]{1,0:T(8,128)(2,1)S(1)}, bf16[1552,128]{1,0:T(8,128)(2,1)S(1)}, u32[]{:S(2)}, u32[]{:S(2)}) collective-permute-start(bf16[1552,128]{1,0:T(8,128)(2,1)S(1)} %collective-permute-done.1.refs_1_), channel_id=1, source_target_pairs={{0,1},{1,2},{2,3},{3,4},{4,5},{5,6},{6,7},{7,8},{8,9},{9,10},{10,1... | collective-permute-start | bytes 1191944 | tf_op jit(solution)/shard_map/ppermute | solution.py:195
  42.3 1.9 %collective-permute-start.3 = (bf16[1552,128]{1,0:T(8,128)(2,1)S(1)}, bf16[1552,128]{1,0:T(8,128)(2,1)S(1)}, u32[]{:S(2)}, u32[]{:S(2)}) collective-permute-start(bf16[1552,128]{1,0:T(8,128)(2,1)S(1)} %collective-permute-done.1.refs_1_), channel_id=1, source_target_pairs={{1,0},{2,1},{3,2},{4,3},{5,4},{6,5},{7,6},{8,7},{9,8},{10,9},{11,1... | collective-permute-start | bytes 1191944 | tf_op jit(solution)/shard_map/ppermute | solution.py:195
  44.3 0.7 pad_maximum_fusion.1
  45.0 5.5 %collective-permute-start.6 = (bf16[784,128]{1,0:T(8,128)(2,1)}, bf16[784,128]{1,0:T(8,128)(2,1)S(1)}, u32[]{:S(2)}, u32[]{:S(2)}) collective-permute-start(bf16[784,128]{1,0:T(8,128)(2,1)} %pad_maximum_fusion.1), channel_id=1, source_target_pairs={{64,0},{128,64},{192,128},{256,192},{320,256},{384,320},{448,384},... | collective-permute-start | bytes 602120 | tf_op jit(solution)/shard_map/ppermute | solution.py:195
  50.5 0.0 collective-permute-done
  50.5 0.4 collective-permute-done.2
  50.9 5.9 %collective-permute-done.3 = bf16[1552,128]{1,0:T(8,128)(2,1)S(1)} collective-permute-done((bf16[1552,128]{1,0:T(8,128)(2,1)S(1)}, bf16[1552,128]{1,0:T(8,128)(2,1)S(1)}, u32[]{:S(2)}, u32[]{:S(2)}) %collective-permute-start.3) | collective-permute-done | bytes 397344 | tf_op jit(solution)/shard_map/ppermute | solution.py:195
  56.8 0.1 broadcast_select_fusion.1
  56.9 22.6 %collective-permute-start.5 = (bf16[1552,128]{1,0:T(8,128)(2,1)S(1)}, bf16[1552,128]{1,0:T(8,128)(2,1)S(1)}, u32[]{:S(2)}, u32[]{:S(2)}) collective-permute-start(bf16[1552,128]{1,0:T(8,128)(2,1)S(1)} %get-tuple-element.5.refs_2_), channel_id=1, source_target_pairs={{1,0},{2,1},{3,2},{4,3},{5,4},{6,5},{7,6},{8,7},{9,8},{10,9},{11,1... | collective-permute-start | bytes 1191944 | tf_op jit(solution)/shard_map/ppermute | solution.py:195
  79.5 20.9 %collective-permute-start.7 = (bf16[784,128]{1,0:T(8,128)(2,1)}, bf16[784,128]{1,0:T(8,128)(2,1)S(1)}, u32[]{:S(2)}, u32[]{:S(2)}) collective-permute-start(bf16[784,128]{1,0:T(8,128)(2,1)} %pad_maximum_fusion.1), channel_id=1, source_target_pairs={{0,0},{64,64},{128,128},{192,192},{256,256},{320,320},{384,384},{4... | collective-permute-start | bytes 602120 | tf_op jit(solution)/shard_map/ppermute | solution.py:195
  100.5 0.0 collective-permute-done.6.refs_4_
  100.5 1.9 %collective-permute-start.9 = (bf16[784,128]{1,0:T(8,128)(2,1)S(1)}, bf16[784,128]{1,0:T(8,128)(2,1)S(1)}, u32[]{:S(2)}, u32[]{:S(2)}) collective-permute-start(bf16[784,128]{1,0:T(8,128)(2,1)S(1)} %collective-permute-done.6.refs_4_), channel_id=1, source_target_pairs={{64,32},{128,96},{192,160},{256,224},{320,288},{384,352},{448,416}... | collective-permute-start | bytes 602120 | tf_op jit(solution)/shard_map/ppermute | solution.py:195
  102.4 0.7 collective-permute-start.8
  103.1 0.7 dynamic-slice_bitcast_fusion.tick_ref
  103.8 0.0 collective-permute-done.7.refs_5_
  103.8 1.3 collective-permute-start.10
  105.1 0.0 collective-permute-done.4
  105.1 0.7 collective-permute-start.11
  105.8 17.4 %collective-permute-done.9.refs_7_ = bf16[784,128]{1,0:T(8,128)(2,1)S(1)} collective-permute-done((bf16[784,128]{1,0:T(8,128)(2,1)S(1)}, bf16[784,128]{1,0:T(8,128)(2,1)S(1)}, u32[]{:S(2)}, u32[]{:S(2)}) %collective-permute-start.9) | collective-permute-done | bytes 200736 | tf_op jit(solution)/shard_map/ppermute | solution.py:195
  123.2 1.9 %collective-permute-start.12 = (bf16[784,128]{1,0:T(8,128)(2,1)S(1)}, bf16[784,128]{1,0:T(8,128)(2,1)S(1)}, u32[]{:S(2)}, u32[]{:S(2)}) collective-permute-start(bf16[784,128]{1,0:T(8,128)(2,1)S(1)} %collective-permute-done.9.refs_7_), channel_id=1, source_target_pairs={{1,33},{65,97},{129,161},{193,225},{257,289},{321,353},{385,417},{... | collective-permute-start | bytes 602120 | tf_op jit(solution)/shard_map/ppermute | solution.py:195
  125.1 0.0 collective-permute-done.5
  125.2 0.0 collective-permute-done.10.refs_8_
  125.2 1.3 %collective-permute-done.12.refs_10_ = bf16[784,128]{1,0:T(8,128)(2,1)S(1)} collective-permute-done((bf16[784,128]{1,0:T(8,128)(2,1)S(1)}, bf16[784,128]{1,0:T(8,128)(2,1)S(1)}, u32[]{:S(2)}, u32[]{:S(2)}) %collective-permute-start.12) | collective-permute-done | bytes 200736 | tf_op jit(solution)/shard_map/ppermute | solution.py:195
  126.5 5.0 %shard_map.73 = bf16[1024,512]{1,0:T(8,128)(2,1)} custom-call(s32[8]{0:T(128)S(1)} %dynamic-slice_bitcast_fusion.tick_ref, bf16[1552,128]{1,0:T(8,128)(2,1)S(1)} %get-tuple-element.6.refs_0_, bf16[1552,128]{1,0:T(8,128)(2,1)S(1)} %collective-permute-done.1.refs_1_, bf16[1552,128]{1,0:T(8,128)(2,1)S(1)} %get-tuple-element.5.refs_2_, ...), custom_call_target="tpu_custom_call" | custom-call | tf_op jit(solution)/shard_map/pallas_call | solution.py:171
  (14 shorter events, 0.1 us)
Async XLA Ops:
  0.0 0.7 copy-start.1
  0.7 43.5 %copy-start = (bf16[1,1,1,6,128,128]{5,4,3,2,1,0:T(8,128)(2,1)S(1)}, bf16[1,1,1,6,128,128]{5,4,3,2,1,0:T(8,128)(2,1)}, u32[]{:S(2)}) copy-start(bf16[1,1,1,6,128,128]{5,4,3,2,1,0:T(8,128)(2,1)} %param.10) | copy-start | bytes 589828
  1.8 11.7 %copy-start.2 = (s32[1,1,1,2,6]{4,3,2,1,0:T(2,128)S(1)}, s32[1,1,1,2,6]{4,3,2,1,0:T(2,128)}, u32[]{:S(2)}) copy-start(s32[1,1,1,2,6]{4,3,2,1,0:T(2,128)} %param.11) | copy-start | bytes 148
  1.8 37.0 %collective-permute-start.1 = (bf16[1552,128]{1,0:T(8,128)(2,1)S(1)}, bf16[1552,128]{1,0:T(8,128)(2,1)S(1)}, u32[]{:S(2)}, u32[]{:S(2)}) collective-permute-start(bf16[1552,128]{1,0:T(8,128)(2,1)S(1)} %pad_maximum_fusion), channel_id=1, source_target_pairs={{1,0},{2,1},{3,2},{4,3},{5,4},{6,5},{7,6},{8,7},{9,8},{10,9},{11,1... | collective-permute-start | bytes 1191944 | tf_op jit(solution)/shard_map/ppermute | solution.py:195
  11.5 39.0 %collective-permute-start = (bf16[1552,128]{1,0:T(8,128)(2,1)S(1)}, bf16[1552,128]{1,0:T(8,128)(2,1)S(1)}, u32[]{:S(2)}, u32[]{:S(2)}) collective-permute-start(bf16[1552,128]{1,0:T(8,128)(2,1)S(1)} %pad_maximum_fusion), channel_id=1, source_target_pairs={{0,0},{1,31},{33,32},{34,63},{66,64},{67,95},{99,96},{100,127},{13... | collective-permute-start | bytes 1191944 | tf_op jit(solution)/shard_map/ppermute | solution.py:195
  12.2 92.9 %collective-permute-start.4 = (bf16[1552,128]{1,0:T(8,128)(2,1)S(1)}, bf16[1552,128]{1,0:T(8,128)(2,1)S(1)}, u32[]{:S(2)}, u32[]{:S(2)}) collective-permute-start(bf16[1552,128]{1,0:T(8,128)(2,1)S(1)} %pad_maximum_fusion), channel_id=1, source_target_pairs={{1,30},{2,31},{34,62},{35,63},{67,94},{68,95},{100,126},{101,127},... | collective-permute-start | bytes 1191944 | tf_op jit(solution)/shard_map/ppermute | solution.py:195
  38.8 12.1 %collective-permute-start.2 = (bf16[1552,128]{1,0:T(8,128)(2,1)S(1)}, bf16[1552,128]{1,0:T(8,128)(2,1)S(1)}, u32[]{:S(2)}, u32[]{:S(2)}) collective-permute-start(bf16[1552,128]{1,0:T(8,128)(2,1)S(1)} %collective-permute-done.1.refs_1_), channel_id=1, source_target_pairs={{0,1},{1,2},{2,3},{3,4},{4,5},{5,6},{6,7},{7,8},{8,9},{9,10},{10,1... | collective-permute-start | bytes 1191944 | tf_op jit(solution)/shard_map/ppermute | solution.py:195
  42.3 14.5 %collective-permute-start.3 = (bf16[1552,128]{1,0:T(8,128)(2,1)S(1)}, bf16[1552,128]{1,0:T(8,128)(2,1)S(1)}, u32[]{:S(2)}, u32[]{:S(2)}) collective-permute-start(bf16[1552,128]{1,0:T(8,128)(2,1)S(1)} %collective-permute-done.1.refs_1_), channel_id=1, source_target_pairs={{1,0},{2,1},{3,2},{4,3},{5,4},{6,5},{7,6},{8,7},{9,8},{10,9},{11,1... | collective-permute-start | bytes 1191944 | tf_op jit(solution)/shard_map/ppermute | solution.py:195
  45.0 55.5 %collective-permute-start.6 = (bf16[784,128]{1,0:T(8,128)(2,1)}, bf16[784,128]{1,0:T(8,128)(2,1)S(1)}, u32[]{:S(2)}, u32[]{:S(2)}) collective-permute-start(bf16[784,128]{1,0:T(8,128)(2,1)} %pad_maximum_fusion.1), channel_id=1, source_target_pairs={{64,0},{128,64},{192,128},{256,192},{320,256},{384,320},{448,384},... | collective-permute-start | bytes 602120 | tf_op jit(solution)/shard_map/ppermute | solution.py:195
  56.9 68.2 %collective-permute-start.5 = (bf16[1552,128]{1,0:T(8,128)(2,1)S(1)}, bf16[1552,128]{1,0:T(8,128)(2,1)S(1)}, u32[]{:S(2)}, u32[]{:S(2)}) collective-permute-start(bf16[1552,128]{1,0:T(8,128)(2,1)S(1)} %get-tuple-element.5.refs_2_), channel_id=1, source_target_pairs={{1,0},{2,1},{3,2},{4,3},{5,4},{6,5},{7,6},{8,7},{9,8},{10,9},{11,1... | collective-permute-start | bytes 1191944 | tf_op jit(solution)/shard_map/ppermute | solution.py:195
  79.5 24.3 %collective-permute-start.7 = (bf16[784,128]{1,0:T(8,128)(2,1)}, bf16[784,128]{1,0:T(8,128)(2,1)S(1)}, u32[]{:S(2)}, u32[]{:S(2)}) collective-permute-start(bf16[784,128]{1,0:T(8,128)(2,1)} %pad_maximum_fusion.1), channel_id=1, source_target_pairs={{0,0},{64,64},{128,128},{192,192},{256,256},{320,320},{384,384},{4... | collective-permute-start | bytes 602120 | tf_op jit(solution)/shard_map/ppermute | solution.py:195
  100.5 22.7 %collective-permute-start.9 = (bf16[784,128]{1,0:T(8,128)(2,1)S(1)}, bf16[784,128]{1,0:T(8,128)(2,1)S(1)}, u32[]{:S(2)}, u32[]{:S(2)}) collective-permute-start(bf16[784,128]{1,0:T(8,128)(2,1)S(1)} %collective-permute-done.6.refs_4_), channel_id=1, source_target_pairs={{64,32},{128,96},{192,160},{256,224},{320,288},{384,352},{448,416}... | collective-permute-start | bytes 602120 | tf_op jit(solution)/shard_map/ppermute | solution.py:195
  102.4 22.8 %collective-permute-start.8 = (bf16[784,128]{1,0:T(8,128)(2,1)}, bf16[784,128]{1,0:T(8,128)(2,1)S(1)}, u32[]{:S(2)}, u32[]{:S(2)}) collective-permute-start(bf16[784,128]{1,0:T(8,128)(2,1)} %pad_maximum_fusion.1), channel_id=1, source_target_pairs={{326,38},{390,102},{454,166},{518,230},{582,294},{646,358},{710,42... | collective-permute-start | bytes 602120 | tf_op jit(solution)/shard_map/ppermute | solution.py:195
  103.8 21.3 %collective-permute-start.10 = (bf16[784,128]{1,0:T(8,128)(2,1)S(1)}, bf16[784,128]{1,0:T(8,128)(2,1)S(1)}, u32[]{:S(2)}, u32[]{:S(2)}) collective-permute-start(bf16[784,128]{1,0:T(8,128)(2,1)S(1)} %collective-permute-done.6.refs_4_), channel_id=1, source_target_pairs={{32,0},{96,64},{160,128},{224,192},{288,256},{352,320},{416,384},{... | collective-permute-start | bytes 602120 | tf_op jit(solution)/shard_map/ppermute | solution.py:195
  105.1 20.1 %collective-permute-start.11 = (bf16[784,128]{1,0:T(8,128)(2,1)S(1)}, bf16[784,128]{1,0:T(8,128)(2,1)S(1)}, u32[]{:S(2)}, u32[]{:S(2)}) collective-permute-start(bf16[784,128]{1,0:T(8,128)(2,1)S(1)} %collective-permute-done.7.refs_5_), channel_id=1, source_target_pairs={{32,0},{96,64},{160,128},{224,192},{288,256},{352,320},{416,384},{... | collective-permute-start | bytes 602120 | tf_op jit(solution)/shard_map/ppermute | solution.py:195
  123.2 3.3 %collective-permute-start.12 = (bf16[784,128]{1,0:T(8,128)(2,1)S(1)}, bf16[784,128]{1,0:T(8,128)(2,1)S(1)}, u32[]{:S(2)}, u32[]{:S(2)}) collective-permute-start(bf16[784,128]{1,0:T(8,128)(2,1)S(1)} %collective-permute-done.9.refs_7_), channel_id=1, source_target_pairs={{1,33},{65,97},{129,161},{193,225},{257,289},{321,353},{385,417},{... | collective-permute-start | bytes 602120 | tf_op jit(solution)/shard_map/ppermute | solution.py:195

commit v2 on v1

v2 whole, which is shorter than its diff:
```python
import jax
import jax.numpy as jnp
import numpy as np
from jax import lax
from jax.experimental import pallas as pl
from jax.experimental.pallas import tpu as pltpu
from jax.sharding import PartitionSpec as P

BLOCK = 128
KR = 8
KC = 4
TICKS = 4
SA = 12
SB = 6
GRID = 32
CHIPS = GRID // 2
TAG = 16
AXES = ("row", "col")

ROLES = {
    (0, 0): {"first": "F", "near": "O", "relay": "H"},
    (0, 1): {"first": "O", "near": "H", "relay": "F"},
    (0, 2): {"first": "F", "near": "H", "relay": "O"},
    (0, 3): {"first": "O", "near": "F", "relay": "H"},
    (1, 0): {"first": "F", "near": "H", "relay": "O"},
    (1, 1): {"first": "O", "near": "H", "relay": "F"},
    (1, 2): {"first": "F", "near": "O", "relay": "H"},
    (1, 3): {"first": "O", "near": "F", "relay": "H"},
}
MOVES = ("first", "near", "relay")
SWAPS = ("first", "late")
RIGHTS = len(MOVES) + len(SWAPS)
LEFTS = TICKS + 2


def offset_of(role, p):
    return {"F": 1, "O": 2 * p, "H": 2 - 2 * p}[role]


def tick_of(role, p, c):
    if role == "F":
        return 2 - p
    if role == "O":
        return 3 * p
    return (3 - 3 * p) if c != p else -1


def tick_of_swap(role, p, c):
    if role == "F":
        return 3 - 2 * c - p
    return 1 + p if c == p else -1


def plan():
    pairs = {name: [] for name in MOVES}
    swaps = {name: [] for name in SWAPS}
    ticks = np.full((2, 2, 4, 8), -1, np.int32)
    for j in range(GRID):
        shift, p = j // 2, j % 2
        d = shift % 4
        roles = ROLES[p, d]
        for c in range(2):
            for at, name in enumerate(MOVES):
                if name in roles:
                    ticks[p, c, d, at] = tick_of(roles[name], p, c)
            late = roles["near"] if roles["relay"] == "H" else roles["relay"]
            for at, role in enumerate((roles["first"], late)):
                ticks[p, c, d, len(MOVES) + at] = tick_of_swap(role, p, c)
            for chip in range(CHIPS):
                here = (2 * chip + c) * GRID + j
                for at, name in enumerate(MOVES):
                    if ticks[p, c, d, at] < 0:
                        continue
                    role = roles[name]
                    core = 1 - c if role == "H" else c
                    if name == "relay" and d != 3:
                        source = chip + offset_of(role, p) - offset_of(roles["first"], p)
                    else:
                        source = chip + shift + offset_of(role, p)
                    source = (2 * (source % CHIPS) + core) * GRID + j
                    pairs[name].append((source, here))
                for at, name in enumerate(SWAPS):
                    if ticks[p, c, d, len(MOVES) + at] >= 0:
                        swaps[name].append(((2 * chip + 1 - c) * GRID + j, here))
    table = np.full((2, GRID, 16), -1, np.int32)
    for c in range(2):
        for j in range(GRID):
            table[c, j, :8] = ticks[j % 2, c, j // 2 % 4]
            lefts = [0, 1, 2, 3, -2, -2]
            if j == 0:
                lefts[0], lefts[4] = -2, 0
            if j == GRID - 1:
                lefts[2], lefts[4] = -2, 2
            if j >= GRID - 2:
                lefts[3], lefts[5] = -2, 3
            table[c, j, 8 : 8 + LEFTS] = lefts
    return pairs, swaps, table


def left_plan():
    skew, before, after, after2 = [], [], [], []
    wrap, wrap2 = [], []
    for i in range(GRID):
        at = lambda col: i * GRID + col % GRID
        for j in range(GRID):
            skew.append((at(i + j + 1), at(j)))
            if j > 0:
                before.append((at(j - 1), at(j)))
            if j < GRID - 1:
                after.append((at(j + 1), at(j)))
            if j < GRID - 2:
                after2.append((at(j + 2), at(j)))
        wrap += [(at(i), at(0)), (at(i + 1), at(GRID - 1))]
        wrap2 += [(at(i + 1), at(GRID - 2)), (at(i + 2), at(GRID - 1))]
    return skew, before, after, after2, wrap, wrap2


def tag(index, count, empty_row, empty_column):
    slots = index.shape[1]
    live = jnp.arange(slots, dtype=jnp.int32) < count
    empty = jnp.array([[empty_row], [empty_column]], jnp.int32)
    places = jnp.where(live[None, :], index, empty).astype(jnp.bfloat16)
    return jnp.pad(places, ((0, TAG - 2), (0, BLOCK - slots)))


def join(upper, lower):
    def copy(upper_ref, lower_ref, out_ref):
        rows = upper_ref.shape[0]
        out_ref[:rows, :] = upper_ref[...]
        out_ref[rows:, :] = lower_ref[...]

    vmem = pl.BlockSpec(memory_space=pltpu.VMEM)
    size = upper.size + lower.size
    return pl.pallas_call(
        copy,
        out_shape=jax.ShapeDtypeStruct((upper.shape[0] + lower.shape[0], BLOCK), upper.dtype),
        in_specs=[vmem, vmem],
        out_specs=vmem,
        cost_estimate=pl.CostEstimate(flops=5 * 10**9, bytes_accessed=4 * size, transcendentals=0),
    )(upper, lower)


def kernel(tick_ref, *refs):
    a_refs = refs[:LEFTS]
    b_refs = refs[LEFTS : LEFTS + RIGHTS]
    out_ref, acc, tags, scal, sem = refs[LEFTS + RIGHTS :]
    for n, (ref, rows) in enumerate([(ref, SA * BLOCK) for ref in a_refs] + [(ref, SB * BLOCK) for ref in b_refs]):
        tags[n] = ref[rows : rows + TAG, :].astype(jnp.float32)[:8].astype(jnp.int32)
    copy = pltpu.make_async_copy(tags, scal, sem)
    copy.start()
    acc[...] = jnp.zeros_like(acc)
    copy.wait()

    def multiply(a, b):
        a_ref, b_ref = a_refs[a], b_refs[b]

        def slot(u, carry):
            row = scal[LEFTS + b, 0, u]
            hits = jnp.int32(0)
            for s in range(SA):
                hits = hits | jnp.where(scal[a, 1, s] == row, 1 << s, 0)

            @pl.when(hits != 0)
            def _():
                right = b_ref[pl.ds(pl.multiple_of(u * BLOCK, BLOCK), BLOCK), :]
                column = scal[LEFTS + b, 1, u]

                def product(s, carry):
                    @pl.when((hits >> s) & 1 == 1)
                    def _():
                        left = a_ref[pl.ds(pl.multiple_of(s * BLOCK, BLOCK), BLOCK), :]
                        place = scal[a, 0, s] * KC + column
                        acc[place] += jnp.dot(left, right, preferred_element_type=jnp.float32)

                    return carry

                lax.fori_loop(0, SA, product, 0)

            return carry

        lax.fori_loop(0, SB, slot, 0)

    for b in range(RIGHTS):
        for a in range(LEFTS):
            pl.when(tick_ref[b] == tick_ref[8 + a])(lambda a=a, b=b: multiply(a, b))
    for r in range(KR):
        for c in range(KC):
            out_ref[r * BLOCK : (r + 1) * BLOCK, c * BLOCK : (c + 1) * BLOCK] = acc[r * KC + c].astype(jnp.bfloat16)


def multiply_all(ticks, lefts, rights):
    n = LEFTS + RIGHTS
    return pl.pallas_call(
        kernel,
        out_shape=jax.ShapeDtypeStruct((KR * BLOCK, KC * BLOCK), jnp.bfloat16),
        in_specs=[pl.BlockSpec(memory_space=pltpu.SMEM)] + [pl.BlockSpec(memory_space=pltpu.VMEM)] * n,
        out_specs=pl.BlockSpec(memory_space=pltpu.VMEM),
        scratch_shapes=[
            pltpu.VMEM((KR * KC, BLOCK, BLOCK), jnp.float32),
            pltpu.VMEM((n, 8, BLOCK), jnp.int32),
            pltpu.SMEM((n, 8, BLOCK), jnp.int32),
            pltpu.SemaphoreType.DMA,
        ],
        compiler_params=pltpu.CompilerParams(vmem_limit_bytes=24 * 1024 * 1024),
    )(ticks, *lefts, *rights)


def send(value, route, name):
    with jax.named_scope("send_" + name):
        return lax.ppermute(value, AXES, route)


def local(a_blocks, a_index, a_count, b_blocks, b_index, b_count):
    row_id = lax.axis_index("row")
    col_id = lax.axis_index("col")
    pairs, swap_pairs, table = plan()
    ticks = jnp.asarray(table)[row_id % 2, col_id]
    skew, before, after, after2, wrap, wrap2 = left_plan()
    a_rows = a_blocks.reshape(SA * BLOCK, BLOCK)
    half = SA // 2 * BLOCK
    lower = jnp.concatenate([a_rows[half:], tag(a_index[0, 0], a_count[0, 0], 0, 64)])
    upper = a_rows[:half]
    left = jnp.concatenate([upper, lower])
    right = jnp.concatenate([b_blocks.reshape(SB * BLOCK, BLOCK), tag(b_index[0, 0, 0], b_count[0, 0, 0], 65, 0)])

    opposite = GRID * GRID // 2
    flip = lambda n: (n + opposite) % (2 * opposite)
    lower = send(lower, [(n, flip(n)) for n in range(2 * opposite)], "over")
    upper = send(upper, skew, "upper")
    lower = send(lower, [(flip(s), d) for s, d in skew], "lower")
    moved = {name: send(right, pairs[name], name) for name in MOVES[:2]}
    wrapped = send(left, wrap, "wrap")
    wrapped2 = send(left, wrap2, "wrap2")
    moved["near"], wrapped, wrapped2 = lax.optimization_barrier((moved["near"], wrapped, wrapped2))
    passing = jnp.where(col_id // 2 % 4 == 3, right, moved["first"])
    moved["relay"] = send(passing, pairs["relay"], "relay")
    swap1 = send(moved["first"], swap_pairs["first"], "swap1")
    left1 = join(upper, lower)
    left3 = send(left1, after2, "after2")
    left2 = send(left1, after, "after")
    left0 = send(left1, before, "before")
    use_near = (col_id // 2 % 4 == 3) | (col_id // 2 % 4 == 2 * (col_id % 2))
    swap2 = send(jnp.where(use_near, moved["near"], moved["relay"]), swap_pairs["late"], "swap2")
    lefts = (left0, left1, left2, left3, wrapped, wrapped2)
    return multiply_all(ticks, lefts, [moved[name] for name in MOVES] + [swap1, swap2])


def solution(mesh):
    in_specs = (
        P("row", "col", None, None, None),
        P("row", "col", None, None),
        P("row", "col"),
        P(None, "row", "col", None, None, None),
        P(None, "row", "col", None, None),
        P(None, "row", "col"),
    )
    out_specs = P("row", "col")
    return jax.shard_map(local, mesh=mesh, in_specs=in_specs, out_specs=out_specs, check_vma=False)
```

time: 132 us -> 120 us (0.909)
  the two profiles are of different devices: /device:TPU:23 before, /device:TPU:121 now
where the time goes in v2:
time: 120 us; the launch traced here: 119 us
  starting transfers between devices  83.2 us (69%)
  waiting for transfers between devices  21.8 us (18%)
  Pallas kernels  7.56 us (6%)
  local copies, waits for them, and re-layouts  2.71 us (2%)
  other arithmetic  2.58 us (2%)
  between operations  1.67 us (1%)
    ppermute x13, starting transfers between devices, send(): return lax.ppermute(value, AXES, route)  83.2 us
    ppermute x13, waiting for transfers between devices, send(): return lax.ppermute(value, AXES, route)  21.8 us
    pallas_call x1, Pallas kernels, multiply_all(): pl.pallas_call(kernel, out_shape=jax.ShapeDtypeStruct((KR * BLOCK, KC * B...  5.76 us
  transfers between devices with their start and end apart: 13, of which 4 were waited for; matrix products, arithmetic and copies ran while one was open for 1% of the time, Pallas kernels for 2%

profile of v2, /device:TPU:121, one launch (start us, length us, event | category | flops | bytes accessed | tf_op | source)
XLA Modules:
  0.0 119.5 jit_solution(4723148073779503241)
XLA Ops:
  0.7 0.8 fusion.2
  1.5 0.9 fusion.1
  2.4 16.1 %collective-permute-start.9 = (bf16[784,128]{1,0:T(8,128)(2,1)S(1)}, bf16[784,128]{1,0:T(8,128)(2,1)S(1)}, u32[]{:S(2)}, u32[]{:S(2)}) collective-permute-start(bf16[784,128]{1,0:T(8,128)(2,1)S(1)} %fusion.1), channel_id=1, source_target_pairs={{64,0},{128,64},{192,128},{256,192},{320,256},{384,320},{448,384},... | collective-permute-start | bytes 602120 | tf_op jit(solution)/shard_map/send_first/ppermute | solution.py:210
  19.2 0.0 copy-start.3
  19.3 0.6 copy-done.3
  19.9 0.1 fusion.3
  20.0 3.9 %collective-permute-start.1 = (bf16[784,128]{1,0:T(8,128)(2,1)S(1)}, bf16[784,128]{1,0:T(8,128)(2,1)S(1)}, u32[]{:S(2)}, u32[]{:S(2)}) collective-permute-start(bf16[784,128]{1,0:T(8,128)(2,1)S(1)} %pad_maximum_fusion.1), channel_id=1, source_target_pairs={{0,512},{1,513},{2,514},{3,515},{4,516},{5,517},{6,518},{7,519},{8... | collective-permute-start | bytes 602120 | tf_op jit(solution)/shard_map/send_over/ppermute | solution.py:210
  23.9 0.0 copy-start.1
  24.0 0.8 collective-permute-start.8
  24.8 0.7 collective-permute-start.7
  25.5 1.3 %collective-permute-start.6 = (bf16[784,128]{1,0:T(8,128)(2,1)S(1)}, bf16[784,128]{1,0:T(8,128)(2,1)S(1)}, u32[]{:S(2)}, u32[]{:S(2)}) collective-permute-start(bf16[784,128]{1,0:T(8,128)(2,1)S(1)} %fusion.1), channel_id=1, source_target_pairs={{0,0},{64,64},{128,128},{192,192},{256,256},{320,320},{384,384},{4... | collective-permute-start | bytes 602120 | tf_op jit(solution)/shard_map/send_near/ppermute | solution.py:210
  26.9 17.0 %collective-permute-done.9.refs_6_ = bf16[784,128]{1,0:T(8,128)(2,1)S(1)} collective-permute-done((bf16[784,128]{1,0:T(8,128)(2,1)S(1)}, bf16[784,128]{1,0:T(8,128)(2,1)S(1)}, u32[]{:S(2)}, u32[]{:S(2)}) %collective-permute-start.9) | collective-permute-done | bytes 200736 | tf_op jit(solution)/shard_map/send_first/ppermute | solution.py:210
  43.8 1.9 %collective-permute-start = (bf16[768,128]{1,0:T(8,128)(2,1)S(1)}, bf16[768,128]{1,0:T(8,128)(2,1)S(1)}, u32[]{:S(2)}, u32[]{:S(2)}) collective-permute-start(bf16[768,128]{1,0:T(8,128)(2,1)S(1)} %bitcast.22), channel_id=1, source_target_pairs={{1,0},{2,1},{3,2},{4,3},{5,4},{6,5},{7,6},{8,7},{9,8},{10,9},{11,1... | collective-permute-start | bytes 589832 | tf_op jit(solution)/shard_map/send_upper/ppermute | solution.py:210
  45.7 0.0 collective-permute-done.1
  45.7 1.9 %collective-permute-start.2 = (bf16[784,128]{1,0:T(8,128)(2,1)S(1)}, bf16[784,128]{1,0:T(8,128)(2,1)S(1)}, u32[]{:S(2)}, u32[]{:S(2)}) collective-permute-start(bf16[784,128]{1,0:T(8,128)(2,1)S(1)} %collective-permute-done.1), channel_id=1, source_target_pairs={{513,0},{514,1},{515,2},{516,3},{517,4},{518,5},{519,6},{520,7},{5... | collective-permute-start | bytes 602120 | tf_op jit(solution)/shard_map/send_lower/ppermute | solution.py:210
  47.7 0.1 broadcast_select_fusion.1
  47.8 0.0 collective-permute-done.6.refs_7_
  47.8 11.1 %collective-permute-start.10 = (bf16[784,128]{1,0:T(8,128)(2,1)S(1)}, bf16[784,128]{1,0:T(8,128)(2,1)S(1)}, u32[]{:S(2)}, u32[]{:S(2)}) collective-permute-start(bf16[784,128]{1,0:T(8,128)(2,1)S(1)} %broadcast_select_fusion.1), channel_id=1, source_target_pairs={{64,32},{128,96},{192,160},{256,224},{320,288},{384,352},{448,416}... | collective-permute-start | bytes 602120 | tf_op jit(solution)/shard_map/send_relay/ppermute | solution.py:210
  58.9 18.9 %collective-permute-start.11 = (bf16[784,128]{1,0:T(8,128)(2,1)S(1)}, bf16[784,128]{1,0:T(8,128)(2,1)S(1)}, u32[]{:S(2)}, u32[]{:S(2)}) collective-permute-start(bf16[784,128]{1,0:T(8,128)(2,1)S(1)} %collective-permute-done.9.refs_6_), channel_id=1, source_target_pairs={{32,0},{96,64},{160,128},{224,192},{288,256},{352,320},{416,384},{... | collective-permute-start | bytes 602120 | tf_op jit(solution)/shard_map/send_swap1/ppermute | solution.py:210
  77.8 0.7 copy-done.6
  78.5 0.7 copy-done.5
  79.1 1.8 %shard_map.91.refs_1_ = bf16[1552,128]{1,0:T(8,128)(2,1)} custom-call(bf16[768,128]{1,0:T(8,128)(2,1)} %copy-done.6, bf16[784,128]{1,0:T(8,128)(2,1)} %copy-done.5), custom_call_target="tpu_custom_call" | custom-call | flops 5000000000 | bytes 794624 | tf_op jit(solution)/shard_map/pallas_call | solution.py:134
  80.9 20.0 %collective-permute-start.5 = (bf16[1552,128]{1,0:T(8,128)(2,1)}, bf16[1552,128]{1,0:T(8,128)(2,1)S(1)}, u32[]{:S(2)}, u32[]{:S(2)}) collective-permute-start(bf16[1552,128]{1,0:T(8,128)(2,1)} %shard_map.91.refs_1_), channel_id=1, source_target_pairs={{2,0},{3,1},{4,2},{5,3},{6,4},{7,5},{8,6},{9,7},{10,8},{11,9},{12,... | collective-permute-start | bytes 1191944 | tf_op jit(solution)/shard_map/send_after2/ppermute | solution.py:210
  100.9 1.9 %collective-permute-start.4 = (bf16[1552,128]{1,0:T(8,128)(2,1)}, bf16[1552,128]{1,0:T(8,128)(2,1)S(1)}, u32[]{:S(2)}, u32[]{:S(2)}) collective-permute-start(bf16[1552,128]{1,0:T(8,128)(2,1)} %shard_map.91.refs_1_), channel_id=1, source_target_pairs={{1,0},{2,1},{3,2},{4,3},{5,4},{6,5},{7,6},{8,7},{9,8},{10,9},{11,1... | collective-permute-start | bytes 1191944 | tf_op jit(solution)/shard_map/send_after/ppermute | solution.py:210
  102.8 3.4 %collective-permute-start.3 = (bf16[1552,128]{1,0:T(8,128)(2,1)}, bf16[1552,128]{1,0:T(8,128)(2,1)S(1)}, u32[]{:S(2)}, u32[]{:S(2)}) collective-permute-start(bf16[1552,128]{1,0:T(8,128)(2,1)} %shard_map.91.refs_1_), channel_id=1, source_target_pairs={{0,1},{1,2},{2,3},{3,4},{4,5},{5,6},{6,7},{7,8},{8,9},{9,10},{10,1... | collective-permute-start | bytes 1191944 | tf_op jit(solution)/shard_map/send_before/ppermute | solution.py:210
  106.2 0.7 broadcast_select_fusion
  106.9 1.3 %collective-permute-start.12 = (bf16[784,128]{1,0:T(8,128)(2,1)}, bf16[784,128]{1,0:T(8,128)(2,1)S(1)}, u32[]{:S(2)}, u32[]{:S(2)}) collective-permute-start(bf16[784,128]{1,0:T(8,128)(2,1)} %broadcast_select_fusion), channel_id=1, source_target_pairs={{32,0},{96,64},{160,128},{224,192},{288,256},{352,320},{416,384},{... | collective-permute-start | bytes 602120 | tf_op jit(solution)/shard_map/send_swap2/ppermute | solution.py:210
  108.2 0.7 dynamic-slice_bitcast_fusion.tick_ref
  108.9 0.5 collective-permute-done.12.refs_10_
  109.4 0.8 collective-permute-done.4.refs_2_
  110.2 3.5 %collective-permute-done.3.refs_0_ = bf16[1552,128]{1,0:T(8,128)(2,1)S(1)} collective-permute-done((bf16[1552,128]{1,0:T(8,128)(2,1)}, bf16[1552,128]{1,0:T(8,128)(2,1)S(1)}, u32[]{:S(2)}, u32[]{:S(2)}) %collective-permute-start.3) | collective-permute-done | bytes 397344 | tf_op jit(solution)/shard_map/send_before/ppermute | solution.py:210
  113.7 5.8 %shard_map.92 = bf16[1024,512]{1,0:T(8,128)(2,1)} custom-call(s32[16]{0:T(128)S(1)} %dynamic-slice_bitcast_fusion.tick_ref, bf16[1552,128]{1,0:T(8,128)(2,1)S(1)} %collective-permute-done.3.refs_0_, bf16[1552,128]{1,0:T(8,128)(2,1)S(1)} %copy-done, bf16[1552,128]{1,0:T(8,128)(2,1)S(1)} %collective-permute-done.4.refs_2_, ...), custom_call_target="tpu_custom_call" | custom-call | tf_op jit(solution)/shard_map/pallas_call | solution.py:193
  (23 shorter events, 0.1 us)
Async XLA Ops:
  0.0 0.7 copy-start.4
  0.0 19.2 %copy-start.2 = (bf16[1,1,12,128,128]{4,3,2,1,0:T(8,128)(2,1)S(1)}, bf16[1,1,12,128,128]{4,3,2,1,0:T(8,128)(2,1)}, u32[]{:S(2)}) copy-start(bf16[1,1,12,128,128]{4,3,2,1,0:T(8,128)(2,1)} %param.9) | copy-start | bytes 1179652
  2.4 41.4 %collective-permute-start.9 = (bf16[784,128]{1,0:T(8,128)(2,1)S(1)}, bf16[784,128]{1,0:T(8,128)(2,1)S(1)}, u32[]{:S(2)}, u32[]{:S(2)}) collective-permute-start(bf16[784,128]{1,0:T(8,128)(2,1)S(1)} %fusion.1), channel_id=1, source_target_pairs={{64,0},{128,64},{192,128},{256,192},{320,256},{384,320},{448,384},... | collective-permute-start | bytes 602120 | tf_op jit(solution)/shard_map/send_first/ppermute | solution.py:210
  19.2 0.7 copy-start.3
  20.0 25.7 %collective-permute-start.1 = (bf16[784,128]{1,0:T(8,128)(2,1)S(1)}, bf16[784,128]{1,0:T(8,128)(2,1)S(1)}, u32[]{:S(2)}, u32[]{:S(2)}) collective-permute-start(bf16[784,128]{1,0:T(8,128)(2,1)S(1)} %pad_maximum_fusion.1), channel_id=1, source_target_pairs={{0,512},{1,513},{2,514},{3,515},{4,516},{5,517},{6,518},{7,519},{8... | collective-permute-start | bytes 602120 | tf_op jit(solution)/shard_map/send_over/ppermute | solution.py:210
  23.9 23.7 %copy-start.1 = (bf16[1,1,1,6,128,128]{5,4,3,2,1,0:T(8,128)(2,1)S(1)}, bf16[1,1,1,6,128,128]{5,4,3,2,1,0:T(8,128)(2,1)}, u32[]{:S(2)}) copy-start(bf16[1,1,1,6,128,128]{5,4,3,2,1,0:T(8,128)(2,1)} %param.12) | copy-start | bytes 589828
  24.0 34.9 %collective-permute-start.8 = (bf16[1552,128]{1,0:T(8,128)(2,1)S(1)}, bf16[1552,128]{1,0:T(8,128)(2,1)S(1)}, u32[]{:S(2)}, u32[]{:S(2)}) collective-permute-start(bf16[1552,128]{1,0:T(8,128)(2,1)S(1)} %pad_maximum_fusion), channel_id=1, source_target_pairs={{1,30},{2,31},{34,62},{35,63},{67,94},{68,95},{100,126},{101,127},... | collective-permute-start | bytes 1191944 | tf_op jit(solution)/shard_map/send_wrap2/ppermute | solution.py:210
  24.8 52.9 %collective-permute-start.7 = (bf16[1552,128]{1,0:T(8,128)(2,1)S(1)}, bf16[1552,128]{1,0:T(8,128)(2,1)S(1)}, u32[]{:S(2)}, u32[]{:S(2)}) collective-permute-start(bf16[1552,128]{1,0:T(8,128)(2,1)S(1)} %pad_maximum_fusion), channel_id=1, source_target_pairs={{0,0},{1,31},{33,32},{34,63},{66,64},{67,95},{99,96},{100,127},{13... | collective-permute-start | bytes 1191944 | tf_op jit(solution)/shard_map/send_wrap/ppermute | solution.py:210
  25.5 22.2 %collective-permute-start.6 = (bf16[784,128]{1,0:T(8,128)(2,1)S(1)}, bf16[784,128]{1,0:T(8,128)(2,1)S(1)}, u32[]{:S(2)}, u32[]{:S(2)}) collective-permute-start(bf16[784,128]{1,0:T(8,128)(2,1)S(1)} %fusion.1), channel_id=1, source_target_pairs={{0,0},{64,64},{128,128},{192,192},{256,256},{320,320},{384,384},{4... | collective-permute-start | bytes 602120 | tf_op jit(solution)/shard_map/send_near/ppermute | solution.py:210
  43.8 34.0 %collective-permute-start = (bf16[768,128]{1,0:T(8,128)(2,1)S(1)}, bf16[768,128]{1,0:T(8,128)(2,1)S(1)}, u32[]{:S(2)}, u32[]{:S(2)}) collective-permute-start(bf16[768,128]{1,0:T(8,128)(2,1)S(1)} %bitcast.22), channel_id=1, source_target_pairs={{1,0},{2,1},{3,2},{4,3},{5,4},{6,5},{7,6},{8,7},{9,8},{10,9},{11,1... | collective-permute-start | bytes 589832 | tf_op jit(solution)/shard_map/send_upper/ppermute | solution.py:210
  45.7 32.0 %collective-permute-start.2 = (bf16[784,128]{1,0:T(8,128)(2,1)S(1)}, bf16[784,128]{1,0:T(8,128)(2,1)S(1)}, u32[]{:S(2)}, u32[]{:S(2)}) collective-permute-start(bf16[784,128]{1,0:T(8,128)(2,1)S(1)} %collective-permute-done.1), channel_id=1, source_target_pairs={{513,0},{514,1},{515,2},{516,3},{517,4},{518,5},{519,6},{520,7},{5... | collective-permute-start | bytes 602120 | tf_op jit(solution)/shard_map/send_lower/ppermute | solution.py:210
  47.8 58.4 %collective-permute-start.10 = (bf16[784,128]{1,0:T(8,128)(2,1)S(1)}, bf16[784,128]{1,0:T(8,128)(2,1)S(1)}, u32[]{:S(2)}, u32[]{:S(2)}) collective-permute-start(bf16[784,128]{1,0:T(8,128)(2,1)S(1)} %broadcast_select_fusion.1), channel_id=1, source_target_pairs={{64,32},{128,96},{192,160},{256,224},{320,288},{384,352},{448,416}... | collective-permute-start | bytes 602120 | tf_op jit(solution)/shard_map/send_relay/ppermute | solution.py:210
  58.9 50.0 %collective-permute-start.11 = (bf16[784,128]{1,0:T(8,128)(2,1)S(1)}, bf16[784,128]{1,0:T(8,128)(2,1)S(1)}, u32[]{:S(2)}, u32[]{:S(2)}) collective-permute-start(bf16[784,128]{1,0:T(8,128)(2,1)S(1)} %collective-permute-done.9.refs_6_), channel_id=1, source_target_pairs={{32,0},{96,64},{160,128},{224,192},{288,256},{352,320},{416,384},{... | collective-permute-start | bytes 602120 | tf_op jit(solution)/shard_map/send_swap1/ppermute | solution.py:210
  77.8 0.7 copy-start.6
  78.5 0.7 copy-start.5
  80.9 32.8 %copy-start = (bf16[1552,128]{1,0:T(8,128)(2,1)S(1)}, bf16[1552,128]{1,0:T(8,128)(2,1)}, u32[]{:S(2)}) copy-start(bf16[1552,128]{1,0:T(8,128)(2,1)} %shard_map.91.refs_1_) | copy-start | bytes 1191940
  80.9 28.5 %collective-permute-start.5 = (bf16[1552,128]{1,0:T(8,128)(2,1)}, bf16[1552,128]{1,0:T(8,128)(2,1)S(1)}, u32[]{:S(2)}, u32[]{:S(2)}) collective-permute-start(bf16[1552,128]{1,0:T(8,128)(2,1)} %shard_map.91.refs_1_), channel_id=1, source_target_pairs={{2,0},{3,1},{4,2},{5,3},{6,4},{7,5},{8,6},{9,7},{10,8},{11,9},{12,... | collective-permute-start | bytes 1191944 | tf_op jit(solution)/shard_map/send_after2/ppermute | solution.py:210
  100.9 9.3 %collective-permute-start.4 = (bf16[1552,128]{1,0:T(8,128)(2,1)}, bf16[1552,128]{1,0:T(8,128)(2,1)S(1)}, u32[]{:S(2)}, u32[]{:S(2)}) collective-permute-start(bf16[1552,128]{1,0:T(8,128)(2,1)} %shard_map.91.refs_1_), channel_id=1, source_target_pairs={{1,0},{2,1},{3,2},{4,3},{5,4},{6,5},{7,6},{8,7},{9,8},{10,9},{11,1... | collective-permute-start | bytes 1191944 | tf_op jit(solution)/shard_map/send_after/ppermute | solution.py:210
  102.8 10.9 %collective-permute-start.3 = (bf16[1552,128]{1,0:T(8,128)(2,1)}, bf16[1552,128]{1,0:T(8,128)(2,1)S(1)}, u32[]{:S(2)}, u32[]{:S(2)}) collective-permute-start(bf16[1552,128]{1,0:T(8,128)(2,1)} %shard_map.91.refs_1_), channel_id=1, source_target_pairs={{0,1},{1,2},{2,3},{3,4},{4,5},{5,6},{6,7},{7,8},{8,9},{9,10},{10,1... | collective-permute-start | bytes 1191944 | tf_op jit(solution)/shard_map/send_before/ppermute | solution.py:210
  106.9 2.6 %collective-permute-start.12 = (bf16[784,128]{1,0:T(8,128)(2,1)}, bf16[784,128]{1,0:T(8,128)(2,1)S(1)}, u32[]{:S(2)}, u32[]{:S(2)}) collective-permute-start(bf16[784,128]{1,0:T(8,128)(2,1)} %broadcast_select_fusion), channel_id=1, source_target_pairs={{32,0},{96,64},{160,128},{224,192},{288,256},{352,320},{416,384},{... | collective-permute-start | bytes 602120 | tf_op jit(solution)/shard_map/send_swap2/ppermute | solution.py:210

commit v3 on v2

--- a/solution.py
+++ b/solution.py
@@ -145,7 +145,8 @@
     b_refs = refs[LEFTS : LEFTS + RIGHTS]
     out_ref, acc, tags, scal, sem = refs[LEFTS + RIGHTS :]
     for n, (ref, rows) in enumerate([(ref, SA * BLOCK) for ref in a_refs] + [(ref, SB * BLOCK) for ref in b_refs]):
-        tags[n] = ref[rows : rows + TAG, :].astype(jnp.float32)[:8].astype(jnp.int32)
+        tags[2 * n : 2 * n + 2, :] = ref[rows : rows + TAG, :].astype(jnp.float32)[:2].astype(jnp.int32)
+    tags[2 * (LEFTS + RIGHTS) :, :] = jnp.zeros((24 - 2 * (LEFTS + RIGHTS), BLOCK), jnp.int32)
     copy = pltpu.make_async_copy(tags, scal, sem)
     copy.start()
     acc[...] = jnp.zeros_like(acc)
@@ -153,23 +154,24 @@
 
     def multiply(a, b):
         a_ref, b_ref = a_refs[a], b_refs[b]
+        inner = [scal[2 * a + 1, s] for s in range(SA)]
 
         def slot(u, carry):
-            row = scal[LEFTS + b, 0, u]
+            row = scal[2 * (LEFTS + b), u]
             hits = jnp.int32(0)
             for s in range(SA):
-                hits = hits | jnp.where(scal[a, 1, s] == row, 1 << s, 0)
+                hits = hits | jnp.where(inner[s] == row, 1 << s, 0)
 
             @pl.when(hits != 0)
             def _():
                 right = b_ref[pl.ds(pl.multiple_of(u * BLOCK, BLOCK), BLOCK), :]
-                column = scal[LEFTS + b, 1, u]
+                column = scal[2 * (LEFTS + b) + 1, u]
 
                 def product(s, carry):
                     @pl.when((hits >> s) & 1 == 1)
                     def _():
                         left = a_ref[pl.ds(pl.multiple_of(s * BLOCK, BLOCK), BLOCK), :]
-                        place = scal[a, 0, s] * KC + column
+                        place = scal[2 * a, s] * KC + column
                         acc[place] += jnp.dot(left, right, preferred_element_type=jnp.float32)
 
                     return carry
@@ -197,8 +199,8 @@
         out_specs=pl.BlockSpec(memory_space=pltpu.VMEM),
         scratch_shapes=[
             pltpu.VMEM((KR * KC, BLOCK, BLOCK), jnp.float32),
-            pltpu.VMEM((n, 8, BLOCK), jnp.int32),
-            pltpu.SMEM((n, 8, BLOCK), jnp.int32),
+            pltpu.VMEM((24, BLOCK), jnp.int32),
+            pltpu.SMEM((24, BLOCK), jnp.int32),
             pltpu.SemaphoreType.DMA,
         ],
         compiler_params=pltpu.CompilerParams(vmem_limit_bytes=24 * 1024 * 1024),

time: 120 us -> 118 us (0.983)
  Pallas kernels: 7.56 us -> 5.97 us
    pallas_call x1, Pallas kernels: 5.76 us -> 4.17 us  [multiply_all(): pl.pallas_call(kernel, out_shape=jax.ShapeDtypeStruct((KR * BLOCK, KC * B...]
where the time goes in v3:
time: 118 us
  starting transfers between devices  83.2 us (71%)
  waiting for transfers between devices  21.8 us (18%)
  Pallas kernels  5.97 us (5%)
  local copies, waits for them, and re-layouts  2.71 us (2%)
  other arithmetic  2.58 us (2%)
  between operations  1.67 us (1%)
    ppermute x13, starting transfers between devices, send(): return lax.ppermute(value, AXES, route)  83.2 us
    ppermute x13, waiting for transfers between devices, send(): return lax.ppermute(value, AXES, route)  21.8 us
    pallas_call x1, Pallas kernels, multiply_all(): pl.pallas_call(kernel, out_shape=jax.ShapeDtypeStruct((KR * BLOCK, KC * B...  4.17 us
  transfers between devices with their start and end apart: 13, of which 4 were waited for; matrix products, arithmetic and copies ran while one was open for 1% of the time, Pallas kernels for 2%

profile of v3, /device:TPU:121, one launch (start us, length us, event | category | flops | bytes accessed | tf_op | source)
XLA Modules:
  0.0 117.9 jit_solution(17695001775369048274)
XLA Ops:
  0.7 0.8 fusion.2
  1.5 0.9 fusion.1
  2.4 16.1 %collective-permute-start.9 = (bf16[784,128]{1,0:T(8,128)(2,1)S(1)}, bf16[784,128]{1,0:T(8,128)(2,1)S(1)}, u32[]{:S(2)}, u32[]{:S(2)}) collective-permute-start(bf16[784,128]{1,0:T(8,128)(2,1)S(1)} %fusion.1), channel_id=1, source_target_pairs={{64,0},{128,64},{192,128},{256,192},{320,256},{384,320},{448,384},... | collective-permute-start | bytes 602120 | tf_op jit(solution)/shard_map/send_first/ppermute | solution.py:212
  19.2 0.0 copy-start.3
  19.3 0.6 copy-done.3
  19.9 0.1 fusion.3
  20.0 3.9 %collective-permute-start.1 = (bf16[784,128]{1,0:T(8,128)(2,1)S(1)}, bf16[784,128]{1,0:T(8,128)(2,1)S(1)}, u32[]{:S(2)}, u32[]{:S(2)}) collective-permute-start(bf16[784,128]{1,0:T(8,128)(2,1)S(1)} %pad_maximum_fusion.1), channel_id=1, source_target_pairs={{0,512},{1,513},{2,514},{3,515},{4,516},{5,517},{6,518},{7,519},{8... | collective-permute-start | bytes 602120 | tf_op jit(solution)/shard_map/send_over/ppermute | solution.py:212
  23.9 0.0 copy-start.1
  24.0 0.8 collective-permute-start.8
  24.8 0.7 collective-permute-start.7
  25.5 1.3 %collective-permute-start.6 = (bf16[784,128]{1,0:T(8,128)(2,1)S(1)}, bf16[784,128]{1,0:T(8,128)(2,1)S(1)}, u32[]{:S(2)}, u32[]{:S(2)}) collective-permute-start(bf16[784,128]{1,0:T(8,128)(2,1)S(1)} %fusion.1), channel_id=1, source_target_pairs={{0,0},{64,64},{128,128},{192,192},{256,256},{320,320},{384,384},{4... | collective-permute-start | bytes 602120 | tf_op jit(solution)/shard_map/send_near/ppermute | solution.py:212
  26.9 17.0 %collective-permute-done.9.refs_6_ = bf16[784,128]{1,0:T(8,128)(2,1)S(1)} collective-permute-done((bf16[784,128]{1,0:T(8,128)(2,1)S(1)}, bf16[784,128]{1,0:T(8,128)(2,1)S(1)}, u32[]{:S(2)}, u32[]{:S(2)}) %collective-permute-start.9) | collective-permute-done | bytes 200736 | tf_op jit(solution)/shard_map/send_first/ppermute | solution.py:212
  43.8 1.9 %collective-permute-start = (bf16[768,128]{1,0:T(8,128)(2,1)S(1)}, bf16[768,128]{1,0:T(8,128)(2,1)S(1)}, u32[]{:S(2)}, u32[]{:S(2)}) collective-permute-start(bf16[768,128]{1,0:T(8,128)(2,1)S(1)} %bitcast.22), channel_id=1, source_target_pairs={{1,0},{2,1},{3,2},{4,3},{5,4},{6,5},{7,6},{8,7},{9,8},{10,9},{11,1... | collective-permute-start | bytes 589832 | tf_op jit(solution)/shard_map/send_upper/ppermute | solution.py:212
  45.7 1.9 %collective-permute-start.2 = (bf16[784,128]{1,0:T(8,128)(2,1)S(1)}, bf16[784,128]{1,0:T(8,128)(2,1)S(1)}, u32[]{:S(2)}, u32[]{:S(2)}) collective-permute-start(bf16[784,128]{1,0:T(8,128)(2,1)S(1)} %collective-permute-done.1), channel_id=1, source_target_pairs={{513,0},{514,1},{515,2},{516,3},{517,4},{518,5},{519,6},{520,7},{5... | collective-permute-start | bytes 602120 | tf_op jit(solution)/shard_map/send_lower/ppermute | solution.py:212
  47.7 0.1 broadcast_select_fusion.1
  47.8 11.1 %collective-permute-start.10 = (bf16[784,128]{1,0:T(8,128)(2,1)S(1)}, bf16[784,128]{1,0:T(8,128)(2,1)S(1)}, u32[]{:S(2)}, u32[]{:S(2)}) collective-permute-start(bf16[784,128]{1,0:T(8,128)(2,1)S(1)} %broadcast_select_fusion.1), channel_id=1, source_target_pairs={{64,32},{128,96},{192,160},{256,224},{320,288},{384,352},{448,416}... | collective-permute-start | bytes 602120 | tf_op jit(solution)/shard_map/send_relay/ppermute | solution.py:212
  58.9 0.0 collective-permute-done.8.refs_5_
  58.9 18.9 %collective-permute-start.11 = (bf16[784,128]{1,0:T(8,128)(2,1)S(1)}, bf16[784,128]{1,0:T(8,128)(2,1)S(1)}, u32[]{:S(2)}, u32[]{:S(2)}) collective-permute-start(bf16[784,128]{1,0:T(8,128)(2,1)S(1)} %collective-permute-done.9.refs_6_), channel_id=1, source_target_pairs={{32,0},{96,64},{160,128},{224,192},{288,256},{352,320},{416,384},{... | collective-permute-start | bytes 602120 | tf_op jit(solution)/shard_map/send_swap1/ppermute | solution.py:212
  77.8 0.0 collective-permute-done.2.lower_ref
  77.8 0.7 copy-done.6
  78.5 0.7 copy-done.5
  79.1 1.8 %shard_map.91.refs_1_ = bf16[1552,128]{1,0:T(8,128)(2,1)} custom-call(bf16[768,128]{1,0:T(8,128)(2,1)} %copy-done.6, bf16[784,128]{1,0:T(8,128)(2,1)} %copy-done.5), custom_call_target="tpu_custom_call" | custom-call | flops 5000000000 | bytes 794624 | tf_op jit(solution)/shard_map/pallas_call | solution.py:134
  80.9 20.0 %collective-permute-start.5 = (bf16[1552,128]{1,0:T(8,128)(2,1)}, bf16[1552,128]{1,0:T(8,128)(2,1)S(1)}, u32[]{:S(2)}, u32[]{:S(2)}) collective-permute-start(bf16[1552,128]{1,0:T(8,128)(2,1)} %shard_map.91.refs_1_), channel_id=1, source_target_pairs={{2,0},{3,1},{4,2},{5,3},{6,4},{7,5},{8,6},{9,7},{10,8},{11,9},{12,... | collective-permute-start | bytes 1191944 | tf_op jit(solution)/shard_map/send_after2/ppermute | solution.py:212
  100.9 1.9 %collective-permute-start.4 = (bf16[1552,128]{1,0:T(8,128)(2,1)}, bf16[1552,128]{1,0:T(8,128)(2,1)S(1)}, u32[]{:S(2)}, u32[]{:S(2)}) collective-permute-start(bf16[1552,128]{1,0:T(8,128)(2,1)} %shard_map.91.refs_1_), channel_id=1, source_target_pairs={{1,0},{2,1},{3,2},{4,3},{5,4},{6,5},{7,6},{8,7},{9,8},{10,9},{11,1... | collective-permute-start | bytes 1191944 | tf_op jit(solution)/shard_map/send_after/ppermute | solution.py:212
  102.8 3.4 %collective-permute-start.3 = (bf16[1552,128]{1,0:T(8,128)(2,1)}, bf16[1552,128]{1,0:T(8,128)(2,1)S(1)}, u32[]{:S(2)}, u32[]{:S(2)}) collective-permute-start(bf16[1552,128]{1,0:T(8,128)(2,1)} %shard_map.91.refs_1_), channel_id=1, source_target_pairs={{0,1},{1,2},{2,3},{3,4},{4,5},{5,6},{6,7},{7,8},{8,9},{9,10},{10,1... | collective-permute-start | bytes 1191944 | tf_op jit(solution)/shard_map/send_before/ppermute | solution.py:212
  106.2 0.7 broadcast_select_fusion
  106.9 1.3 %collective-permute-start.12 = (bf16[784,128]{1,0:T(8,128)(2,1)}, bf16[784,128]{1,0:T(8,128)(2,1)S(1)}, u32[]{:S(2)}, u32[]{:S(2)}) collective-permute-start(bf16[784,128]{1,0:T(8,128)(2,1)} %broadcast_select_fusion), channel_id=1, source_target_pairs={{32,0},{96,64},{160,128},{224,192},{288,256},{352,320},{416,384},{... | collective-permute-start | bytes 602120 | tf_op jit(solution)/shard_map/send_swap2/ppermute | solution.py:212
  108.2 0.7 dynamic-slice_bitcast_fusion.tick_ref
  108.9 0.5 collective-permute-done.12.refs_10_
  109.4 0.8 collective-permute-done.4.refs_2_
  110.2 3.5 %collective-permute-done.3.refs_0_ = bf16[1552,128]{1,0:T(8,128)(2,1)S(1)} collective-permute-done((bf16[1552,128]{1,0:T(8,128)(2,1)}, bf16[1552,128]{1,0:T(8,128)(2,1)S(1)}, u32[]{:S(2)}, u32[]{:S(2)}) %collective-permute-start.3) | collective-permute-done | bytes 397344 | tf_op jit(solution)/shard_map/send_before/ppermute | solution.py:212
  113.7 4.2 %shard_map.92 = bf16[1024,512]{1,0:T(8,128)(2,1)} custom-call(s32[16]{0:T(128)S(1)} %dynamic-slice_bitcast_fusion.tick_ref, bf16[1552,128]{1,0:T(8,128)(2,1)S(1)} %collective-permute-done.3.refs_0_, bf16[1552,128]{1,0:T(8,128)(2,1)S(1)} %copy-done, bf16[1552,128]{1,0:T(8,128)(2,1)S(1)} %collective-permute-done.4.refs_2_, ...), custom_call_target="tpu_custom_call" | custom-call | tf_op jit(solution)/shard_map/pallas_call | solution.py:195
  (23 shorter events, 0.1 us)
Async XLA Ops:
  0.0 0.7 copy-start.4
  0.0 19.2 %copy-start.2 = (bf16[1,1,12,128,128]{4,3,2,1,0:T(8,128)(2,1)S(1)}, bf16[1,1,12,128,128]{4,3,2,1,0:T(8,128)(2,1)}, u32[]{:S(2)}) copy-start(bf16[1,1,12,128,128]{4,3,2,1,0:T(8,128)(2,1)} %param.9) | copy-start | bytes 1179652
  2.4 41.4 %collective-permute-start.9 = (bf16[784,128]{1,0:T(8,128)(2,1)S(1)}, bf16[784,128]{1,0:T(8,128)(2,1)S(1)}, u32[]{:S(2)}, u32[]{:S(2)}) collective-permute-start(bf16[784,128]{1,0:T(8,128)(2,1)S(1)} %fusion.1), channel_id=1, source_target_pairs={{64,0},{128,64},{192,128},{256,192},{320,256},{384,320},{448,384},... | collective-permute-start | bytes 602120 | tf_op jit(solution)/shard_map/send_first/ppermute | solution.py:212
  19.2 0.7 copy-start.3
  20.0 25.7 %collective-permute-start.1 = (bf16[784,128]{1,0:T(8,128)(2,1)S(1)}, bf16[784,128]{1,0:T(8,128)(2,1)S(1)}, u32[]{:S(2)}, u32[]{:S(2)}) collective-permute-start(bf16[784,128]{1,0:T(8,128)(2,1)S(1)} %pad_maximum_fusion.1), channel_id=1, source_target_pairs={{0,512},{1,513},{2,514},{3,515},{4,516},{5,517},{6,518},{7,519},{8... | collective-permute-start | bytes 602120 | tf_op jit(solution)/shard_map/send_over/ppermute | solution.py:212
  23.9 23.7 %copy-start.1 = (bf16[1,1,1,6,128,128]{5,4,3,2,1,0:T(8,128)(2,1)S(1)}, bf16[1,1,1,6,128,128]{5,4,3,2,1,0:T(8,128)(2,1)}, u32[]{:S(2)}) copy-start(bf16[1,1,1,6,128,128]{5,4,3,2,1,0:T(8,128)(2,1)} %param.12) | copy-start | bytes 589828
  24.0 34.9 %collective-permute-start.8 = (bf16[1552,128]{1,0:T(8,128)(2,1)S(1)}, bf16[1552,128]{1,0:T(8,128)(2,1)S(1)}, u32[]{:S(2)}, u32[]{:S(2)}) collective-permute-start(bf16[1552,128]{1,0:T(8,128)(2,1)S(1)} %pad_maximum_fusion), channel_id=1, source_target_pairs={{1,30},{2,31},{34,62},{35,63},{67,94},{68,95},{100,126},{101,127},... | collective-permute-start | bytes 1191944 | tf_op jit(solution)/shard_map/send_wrap2/ppermute | solution.py:212
  24.8 52.9 %collective-permute-start.7 = (bf16[1552,128]{1,0:T(8,128)(2,1)S(1)}, bf16[1552,128]{1,0:T(8,128)(2,1)S(1)}, u32[]{:S(2)}, u32[]{:S(2)}) collective-permute-start(bf16[1552,128]{1,0:T(8,128)(2,1)S(1)} %pad_maximum_fusion), channel_id=1, source_target_pairs={{0,0},{1,31},{33,32},{34,63},{66,64},{67,95},{99,96},{100,127},{13... | collective-permute-start | bytes 1191944 | tf_op jit(solution)/shard_map/send_wrap/ppermute | solution.py:212
  25.5 22.2 %collective-permute-start.6 = (bf16[784,128]{1,0:T(8,128)(2,1)S(1)}, bf16[784,128]{1,0:T(8,128)(2,1)S(1)}, u32[]{:S(2)}, u32[]{:S(2)}) collective-permute-start(bf16[784,128]{1,0:T(8,128)(2,1)S(1)} %fusion.1), channel_id=1, source_target_pairs={{0,0},{64,64},{128,128},{192,192},{256,256},{320,320},{384,384},{4... | collective-permute-start | bytes 602120 | tf_op jit(solution)/shard_map/send_near/ppermute | solution.py:212
  43.8 34.0 %collective-permute-start = (bf16[768,128]{1,0:T(8,128)(2,1)S(1)}, bf16[768,128]{1,0:T(8,128)(2,1)S(1)}, u32[]{:S(2)}, u32[]{:S(2)}) collective-permute-start(bf16[768,128]{1,0:T(8,128)(2,1)S(1)} %bitcast.22), channel_id=1, source_target_pairs={{1,0},{2,1},{3,2},{4,3},{5,4},{6,5},{7,6},{8,7},{9,8},{10,9},{11,1... | collective-permute-start | bytes 589832 | tf_op jit(solution)/shard_map/send_upper/ppermute | solution.py:212
  45.7 32.0 %collective-permute-start.2 = (bf16[784,128]{1,0:T(8,128)(2,1)S(1)}, bf16[784,128]{1,0:T(8,128)(2,1)S(1)}, u32[]{:S(2)}, u32[]{:S(2)}) collective-permute-start(bf16[784,128]{1,0:T(8,128)(2,1)S(1)} %collective-permute-done.1), channel_id=1, source_target_pairs={{513,0},{514,1},{515,2},{516,3},{517,4},{518,5},{519,6},{520,7},{5... | collective-permute-start | bytes 602120 | tf_op jit(solution)/shard_map/send_lower/ppermute | solution.py:212
  47.8 58.4 %collective-permute-start.10 = (bf16[784,128]{1,0:T(8,128)(2,1)S(1)}, bf16[784,128]{1,0:T(8,128)(2,1)S(1)}, u32[]{:S(2)}, u32[]{:S(2)}) collective-permute-start(bf16[784,128]{1,0:T(8,128)(2,1)S(1)} %broadcast_select_fusion.1), channel_id=1, source_target_pairs={{64,32},{128,96},{192,160},{256,224},{320,288},{384,352},{448,416}... | collective-permute-start | bytes 602120 | tf_op jit(solution)/shard_map/send_relay/ppermute | solution.py:212
  58.9 50.0 %collective-permute-start.11 = (bf16[784,128]{1,0:T(8,128)(2,1)S(1)}, bf16[784,128]{1,0:T(8,128)(2,1)S(1)}, u32[]{:S(2)}, u32[]{:S(2)}) collective-permute-start(bf16[784,128]{1,0:T(8,128)(2,1)S(1)} %collective-permute-done.9.refs_6_), channel_id=1, source_target_pairs={{32,0},{96,64},{160,128},{224,192},{288,256},{352,320},{416,384},{... | collective-permute-start | bytes 602120 | tf_op jit(solution)/shard_map/send_swap1/ppermute | solution.py:212
  77.8 0.7 copy-start.6
  78.5 0.7 copy-start.5
  80.9 32.8 %copy-start = (bf16[1552,128]{1,0:T(8,128)(2,1)S(1)}, bf16[1552,128]{1,0:T(8,128)(2,1)}, u32[]{:S(2)}) copy-start(bf16[1552,128]{1,0:T(8,128)(2,1)} %shard_map.91.refs_1_) | copy-start | bytes 1191940
  80.9 28.5 %collective-permute-start.5 = (bf16[1552,128]{1,0:T(8,128)(2,1)}, bf16[1552,128]{1,0:T(8,128)(2,1)S(1)}, u32[]{:S(2)}, u32[]{:S(2)}) collective-permute-start(bf16[1552,128]{1,0:T(8,128)(2,1)} %shard_map.91.refs_1_), channel_id=1, source_target_pairs={{2,0},{3,1},{4,2},{5,3},{6,4},{7,5},{8,6},{9,7},{10,8},{11,9},{12,... | collective-permute-start | bytes 1191944 | tf_op jit(solution)/shard_map/send_after2/ppermute | solution.py:212
  100.9 9.3 %collective-permute-start.4 = (bf16[1552,128]{1,0:T(8,128)(2,1)}, bf16[1552,128]{1,0:T(8,128)(2,1)S(1)}, u32[]{:S(2)}, u32[]{:S(2)}) collective-permute-start(bf16[1552,128]{1,0:T(8,128)(2,1)} %shard_map.91.refs_1_), channel_id=1, source_target_pairs={{1,0},{2,1},{3,2},{4,3},{5,4},{6,5},{7,6},{8,7},{9,8},{10,9},{11,1... | collective-permute-start | bytes 1191944 | tf_op jit(solution)/shard_map/send_after/ppermute | solution.py:212
  102.8 10.9 %collective-permute-start.3 = (bf16[1552,128]{1,0:T(8,128)(2,1)}, bf16[1552,128]{1,0:T(8,128)(2,1)S(1)}, u32[]{:S(2)}, u32[]{:S(2)}) collective-permute-start(bf16[1552,128]{1,0:T(8,128)(2,1)} %shard_map.91.refs_1_), channel_id=1, source_target_pairs={{0,1},{1,2},{2,3},{3,4},{4,5},{5,6},{6,7},{7,8},{8,9},{9,10},{10,1... | collective-permute-start | bytes 1191944 | tf_op jit(solution)/shard_map/send_before/ppermute | solution.py:212
  106.9 2.6 %collective-permute-start.12 = (bf16[784,128]{1,0:T(8,128)(2,1)}, bf16[784,128]{1,0:T(8,128)(2,1)S(1)}, u32[]{:S(2)}, u32[]{:S(2)}) collective-permute-start(bf16[784,128]{1,0:T(8,128)(2,1)} %broadcast_select_fusion), channel_id=1, source_target_pairs={{32,0},{96,64},{160,128},{224,192},{288,256},{352,320},{416,384},{... | collective-permute-start | bytes 602120 | tf_op jit(solution)/shard_map/send_swap2/ppermute | solution.py:212

commit v4 on v3

--- a/solution.py
+++ b/solution.py
@@ -123,23 +123,6 @@
     return jnp.pad(places, ((0, TAG - 2), (0, BLOCK - slots)))
 
 
-def join(upper, lower):
-    def copy(upper_ref, lower_ref, out_ref):
-        rows = upper_ref.shape[0]
-        out_ref[:rows, :] = upper_ref[...]
-        out_ref[rows:, :] = lower_ref[...]
-
-    vmem = pl.BlockSpec(memory_space=pltpu.VMEM)
-    size = upper.size + lower.size
-    return pl.pallas_call(
-        copy,
-        out_shape=jax.ShapeDtypeStruct((upper.shape[0] + lower.shape[0], BLOCK), upper.dtype),
-        in_specs=[vmem, vmem],
-        out_specs=vmem,
-        cost_estimate=pl.CostEstimate(flops=5 * 10**9, bytes_accessed=4 * size, transcendentals=0),
-    )(upper, lower)
-
-
 def kernel(tick_ref, *refs):
     a_refs = refs[:LEFTS]
     b_refs = refs[LEFTS : LEFTS + RIGHTS]
@@ -237,7 +220,7 @@
     passing = jnp.where(col_id // 2 % 4 == 3, right, moved["first"])
     moved["relay"] = send(passing, pairs["relay"], "relay")
     swap1 = send(moved["first"], swap_pairs["first"], "swap1")
-    left1 = join(upper, lower)
+    left1 = jnp.concatenate([upper, lower])
     left3 = send(left1, after2, "after2")
     left2 = send(left1, after, "after")
     left0 = send(left1, before, "before")

time: 118 us -> 130 us (1.10)
  the two profiles are of different devices: /device:TPU:121 before, /device:TPU:927 now
where the time goes in v4:
time: 130 us; the launch traced here: 129 us
  starting transfers between devices  103 us (79%)
  waiting for transfers between devices  15.9 us (12%)
  Pallas kernels  4.22 us (3%)
  other arithmetic  2.59 us (2%)
  between operations  1.68 us (1%)
  local copies, waits for them, and re-layouts  1.43 us (1%)
    ppermute x13, starting transfers between devices, send(): return lax.ppermute(value, AXES, route)  103 us
    ppermute x13, waiting for transfers between devices, send(): return lax.ppermute(value, AXES, route)  15.9 us
    pallas_call x1, Pallas kernels, multiply_all(): pl.pallas_call(kernel, out_shape=jax.ShapeDtypeStruct((KR * BLOCK, KC * B...  4.22 us
  transfers between devices with their start and end apart: 13, of which 4 were waited for; matrix products, arithmetic and copies ran while one was open for 1% of the time, Pallas kernels for 0%

profile of v4, /device:TPU:927, one launch (start us, length us, event | category | flops | bytes accessed | tf_op | source)
XLA Modules:
  0.0 128.8 jit_solution(9701889592833763126)
XLA Ops:
  0.7 0.8 fusion.2
  1.5 0.9 fusion.1
  2.4 1.9 %collective-permute-start.9 = (bf16[784,128]{1,0:T(8,128)(2,1)S(1)}, bf16[784,128]{1,0:T(8,128)(2,1)S(1)}, u32[]{:S(2)}, u32[]{:S(2)}) collective-permute-start(bf16[784,128]{1,0:T(8,128)(2,1)S(1)} %fusion.1), channel_id=1, source_target_pairs={{64,0},{128,64},{192,128},{256,192},{320,256},{384,320},{448,384},... | collective-permute-start | bytes 602120 | tf_op jit(solution)/shard_map/send_first/ppermute | solution.py:195
  5.0 0.0 copy-start.2
  5.1 0.6 copy-done.2
  5.7 0.1 fusion.3
  5.8 2.9 %collective-permute-start.1 = (bf16[784,128]{1,0:T(8,128)(2,1)S(1)}, bf16[784,128]{1,0:T(8,128)(2,1)S(1)}, u32[]{:S(2)}, u32[]{:S(2)}) collective-permute-start(bf16[784,128]{1,0:T(8,128)(2,1)S(1)} %pad_maximum_fusion.1), channel_id=1, source_target_pairs={{0,512},{1,513},{2,514},{3,515},{4,516},{5,517},{6,518},{7,519},{8... | collective-permute-start | bytes 602120 | tf_op jit(solution)/shard_map/send_over/ppermute | solution.py:195
  8.7 0.0 copy-start
  8.7 0.8 collective-permute-start.8
  9.6 0.7 collective-permute-start.7
  10.3 14.6 %collective-permute-start.6 = (bf16[784,128]{1,0:T(8,128)(2,1)S(1)}, bf16[784,128]{1,0:T(8,128)(2,1)S(1)}, u32[]{:S(2)}, u32[]{:S(2)}) collective-permute-start(bf16[784,128]{1,0:T(8,128)(2,1)S(1)} %fusion.1), channel_id=1, source_target_pairs={{0,0},{64,64},{128,128},{192,192},{256,256},{320,320},{384,384},{4... | collective-permute-start | bytes 602120 | tf_op jit(solution)/shard_map/send_near/ppermute | solution.py:195
  24.9 2.0 %collective-permute-done.9.refs_6_ = bf16[784,128]{1,0:T(8,128)(2,1)S(1)} collective-permute-done((bf16[784,128]{1,0:T(8,128)(2,1)S(1)}, bf16[784,128]{1,0:T(8,128)(2,1)S(1)}, u32[]{:S(2)}, u32[]{:S(2)}) %collective-permute-start.9) | collective-permute-done | bytes 200736 | tf_op jit(solution)/shard_map/send_first/ppermute | solution.py:195
  26.9 0.7 collective-permute-start
  27.6 8.5 %collective-permute-start.2 = (bf16[784,128]{1,0:T(8,128)(2,1)S(1)}, bf16[784,128]{1,0:T(8,128)(2,1)S(1)}, u32[]{:S(2)}, u32[]{:S(2)}) collective-permute-start(bf16[784,128]{1,0:T(8,128)(2,1)S(1)} %collective-permute-done.1), channel_id=1, source_target_pairs={{513,0},{514,1},{515,2},{516,3},{517,4},{518,5},{519,6},{520,7},{5... | collective-permute-start | bytes 602120 | tf_op jit(solution)/shard_map/send_lower/ppermute | solution.py:195
  36.2 0.1 broadcast_select_fusion.1
  36.2 24.7 %collective-permute-start.10 = (bf16[784,128]{1,0:T(8,128)(2,1)S(1)}, bf16[784,128]{1,0:T(8,128)(2,1)S(1)}, u32[]{:S(2)}, u32[]{:S(2)}) collective-permute-start(bf16[784,128]{1,0:T(8,128)(2,1)S(1)} %broadcast_select_fusion.1), channel_id=1, source_target_pairs={{64,32},{128,96},{192,160},{256,224},{320,288},{384,352},{448,416}... | collective-permute-start | bytes 602120 | tf_op jit(solution)/shard_map/send_relay/ppermute | solution.py:195
  61.0 0.0 collective-permute-done.6.refs_7_
  61.0 1.3 %collective-permute-start.11 = (bf16[784,128]{1,0:T(8,128)(2,1)S(1)}, bf16[784,128]{1,0:T(8,128)(2,1)S(1)}, u32[]{:S(2)}, u32[]{:S(2)}) collective-permute-start(bf16[784,128]{1,0:T(8,128)(2,1)S(1)} %collective-permute-done.9.refs_6_), channel_id=1, source_target_pairs={{32,0},{96,64},{160,128},{224,192},{288,256},{352,320},{416,384},{... | collective-permute-start | bytes 602120 | tf_op jit(solution)/shard_map/send_swap1/ppermute | solution.py:195
  62.3 0.0 collective-permute-done.7.refs_4_
  62.3 0.0 collective-permute-done.2
  62.4 36.2 %collective-permute-start.5 = (bf16[1552,128]{1,0:T(8,128)(2,1)S(1)}, bf16[1552,128]{1,0:T(8,128)(2,1)S(1)}, u32[]{:S(2)}, u32[]{:S(2)}) collective-permute-start(bf16[1552,128]{1,0:T(8,128)(2,1)S(1)} %constant_dynamic-update-slice_fusion.refs_1_), channel_id=1, source_target_pairs={{2,0},{3,1},{4,2},{5,3},{6,4},{7,5},{8,6},{9,7},{10,8},{11,9},{12,... | collective-permute-start | bytes 1191944 | tf_op jit(solution)/shard_map/send_after2/ppermute | solution.py:195
  98.6 1.9 %collective-permute-start.4 = (bf16[1552,128]{1,0:T(8,128)(2,1)S(1)}, bf16[1552,128]{1,0:T(8,128)(2,1)S(1)}, u32[]{:S(2)}, u32[]{:S(2)}) collective-permute-start(bf16[1552,128]{1,0:T(8,128)(2,1)S(1)} %constant_dynamic-update-slice_fusion.refs_1_), channel_id=1, source_target_pairs={{1,0},{2,1},{3,2},{4,3},{5,4},{6,5},{7,6},{8,7},{9,8},{10,9},{11,1... | collective-permute-start | bytes 1191944 | tf_op jit(solution)/shard_map/send_after/ppermute | solution.py:195
  100.5 5.5 %collective-permute-start.3 = (bf16[1552,128]{1,0:T(8,128)(2,1)S(1)}, bf16[1552,128]{1,0:T(8,128)(2,1)S(1)}, u32[]{:S(2)}, u32[]{:S(2)}) collective-permute-start(bf16[1552,128]{1,0:T(8,128)(2,1)S(1)} %constant_dynamic-update-slice_fusion.refs_1_), channel_id=1, source_target_pairs={{0,1},{1,2},{2,3},{3,4},{4,5},{5,6},{6,7},{7,8},{8,9},{9,10},{10,1... | collective-permute-start | bytes 1191944 | tf_op jit(solution)/shard_map/send_before/ppermute | solution.py:195
  106.0 0.0 collective-permute-done.10.refs_8_
  106.0 0.7 broadcast_select_fusion
  106.7 3.2 %collective-permute-start.12 = (bf16[784,128]{1,0:T(8,128)(2,1)}, bf16[784,128]{1,0:T(8,128)(2,1)S(1)}, u32[]{:S(2)}, u32[]{:S(2)}) collective-permute-start(bf16[784,128]{1,0:T(8,128)(2,1)} %broadcast_select_fusion), channel_id=1, source_target_pairs={{32,0},{96,64},{160,128},{224,192},{288,256},{352,320},{416,384},{... | collective-permute-start | bytes 602120 | tf_op jit(solution)/shard_map/send_swap2/ppermute | solution.py:195
  110.0 0.7 dynamic-slice_bitcast_fusion.tick_ref
  110.7 0.0 collective-permute-done.11.refs_9_
  110.7 0.5 collective-permute-done.12.refs_10_
  111.2 8.6 %collective-permute-done.4.refs_2_ = bf16[1552,128]{1,0:T(8,128)(2,1)S(1)} collective-permute-done((bf16[1552,128]{1,0:T(8,128)(2,1)S(1)}, bf16[1552,128]{1,0:T(8,128)(2,1)S(1)}, u32[]{:S(2)}, u32[]{:S(2)}) %collective-permute-start.4) | collective-permute-done | bytes 397344 | tf_op jit(solution)/shard_map/send_after/ppermute | solution.py:195
  119.8 4.7 %collective-permute-done.3.refs_0_ = bf16[1552,128]{1,0:T(8,128)(2,1)S(1)} collective-permute-done((bf16[1552,128]{1,0:T(8,128)(2,1)S(1)}, bf16[1552,128]{1,0:T(8,128)(2,1)S(1)}, u32[]{:S(2)}, u32[]{:S(2)}) %collective-permute-start.3) | collective-permute-done | bytes 397344 | tf_op jit(solution)/shard_map/send_before/ppermute | solution.py:195
  124.5 4.2 %shard_map.91 = bf16[1024,512]{1,0:T(8,128)(2,1)} custom-call(s32[16]{0:T(128)S(1)} %dynamic-slice_bitcast_fusion.tick_ref, bf16[1552,128]{1,0:T(8,128)(2,1)S(1)} %collective-permute-done.3.refs_0_, bf16[1552,128]{1,0:T(8,128)(2,1)S(1)} %constant_dynamic-update-slice_fusion.refs_1_, bf16[1552,128]{1,0:T(8,128)(2,1)S(1)} %collective-permute-done.4.refs_2_, ...), custom_call_target="tpu_custom_call" | custom-call | tf_op jit(solution)/shard_map/pallas_call | solution.py:178
  (18 shorter events, 0.2 us)
Async XLA Ops:
  0.0 0.7 copy-start.3
  0.0 5.0 %copy-start.1 = (bf16[1,1,12,128,128]{4,3,2,1,0:T(8,128)(2,1)S(1)}, bf16[1,1,12,128,128]{4,3,2,1,0:T(8,128)(2,1)}, u32[]{:S(2)}) copy-start(bf16[1,1,12,128,128]{4,3,2,1,0:T(8,128)(2,1)} %param.9) | copy-start | bytes 1179652
  2.4 24.5 %collective-permute-start.9 = (bf16[784,128]{1,0:T(8,128)(2,1)S(1)}, bf16[784,128]{1,0:T(8,128)(2,1)S(1)}, u32[]{:S(2)}, u32[]{:S(2)}) collective-permute-start(bf16[784,128]{1,0:T(8,128)(2,1)S(1)} %fusion.1), channel_id=1, source_target_pairs={{64,0},{128,64},{192,128},{256,192},{320,256},{384,320},{448,384},... | collective-permute-start | bytes 602120 | tf_op jit(solution)/shard_map/send_first/ppermute | solution.py:195
  5.0 0.7 copy-start.2
  5.8 21.8 %collective-permute-start.1 = (bf16[784,128]{1,0:T(8,128)(2,1)S(1)}, bf16[784,128]{1,0:T(8,128)(2,1)S(1)}, u32[]{:S(2)}, u32[]{:S(2)}) collective-permute-start(bf16[784,128]{1,0:T(8,128)(2,1)S(1)} %pad_maximum_fusion.1), channel_id=1, source_target_pairs={{0,512},{1,513},{2,514},{3,515},{4,516},{5,517},{6,518},{7,519},{8... | collective-permute-start | bytes 602120 | tf_op jit(solution)/shard_map/send_over/ppermute | solution.py:195
  8.7 27.5 %copy-start = (bf16[1,1,1,6,128,128]{5,4,3,2,1,0:T(8,128)(2,1)S(1)}, bf16[1,1,1,6,128,128]{5,4,3,2,1,0:T(8,128)(2,1)}, u32[]{:S(2)}) copy-start(bf16[1,1,1,6,128,128]{5,4,3,2,1,0:T(8,128)(2,1)} %param.12) | copy-start | bytes 589828
  8.7 53.6 %collective-permute-start.8 = (bf16[1552,128]{1,0:T(8,128)(2,1)S(1)}, bf16[1552,128]{1,0:T(8,128)(2,1)S(1)}, u32[]{:S(2)}, u32[]{:S(2)}) collective-permute-start(bf16[1552,128]{1,0:T(8,128)(2,1)S(1)} %pad_maximum_fusion), channel_id=1, source_target_pairs={{1,30},{2,31},{34,62},{35,63},{67,94},{68,95},{100,126},{101,127},... | collective-permute-start | bytes 1191944 | tf_op jit(solution)/shard_map/send_wrap2/ppermute | solution.py:195
  9.6 52.7 %collective-permute-start.7 = (bf16[1552,128]{1,0:T(8,128)(2,1)S(1)}, bf16[1552,128]{1,0:T(8,128)(2,1)S(1)}, u32[]{:S(2)}, u32[]{:S(2)}) collective-permute-start(bf16[1552,128]{1,0:T(8,128)(2,1)S(1)} %pad_maximum_fusion), channel_id=1, source_target_pairs={{0,0},{1,31},{33,32},{34,63},{66,64},{67,95},{99,96},{100,127},{13... | collective-permute-start | bytes 1191944 | tf_op jit(solution)/shard_map/send_wrap/ppermute | solution.py:195
  10.3 50.7 %collective-permute-start.6 = (bf16[784,128]{1,0:T(8,128)(2,1)S(1)}, bf16[784,128]{1,0:T(8,128)(2,1)S(1)}, u32[]{:S(2)}, u32[]{:S(2)}) collective-permute-start(bf16[784,128]{1,0:T(8,128)(2,1)S(1)} %fusion.1), channel_id=1, source_target_pairs={{0,0},{64,64},{128,128},{192,192},{256,256},{320,320},{384,384},{4... | collective-permute-start | bytes 602120 | tf_op jit(solution)/shard_map/send_near/ppermute | solution.py:195
  26.9 9.3 %collective-permute-start = (bf16[768,128]{1,0:T(8,128)(2,1)S(1)}, bf16[768,128]{1,0:T(8,128)(2,1)S(1)}, u32[]{:S(2)}, u32[]{:S(2)}) collective-permute-start(bf16[768,128]{1,0:T(8,128)(2,1)S(1)} %bitcast.22), channel_id=1, source_target_pairs={{1,0},{2,1},{3,2},{4,3},{5,4},{6,5},{7,6},{8,7},{9,8},{10,9},{11,1... | collective-permute-start | bytes 589832 | tf_op jit(solution)/shard_map/send_upper/ppermute | solution.py:195
  27.6 34.7 %collective-permute-start.2 = (bf16[784,128]{1,0:T(8,128)(2,1)S(1)}, bf16[784,128]{1,0:T(8,128)(2,1)S(1)}, u32[]{:S(2)}, u32[]{:S(2)}) collective-permute-start(bf16[784,128]{1,0:T(8,128)(2,1)S(1)} %collective-permute-done.1), channel_id=1, source_target_pairs={{513,0},{514,1},{515,2},{516,3},{517,4},{518,5},{519,6},{520,7},{5... | collective-permute-start | bytes 602120 | tf_op jit(solution)/shard_map/send_lower/ppermute | solution.py:195
  36.2 69.8 %collective-permute-start.10 = (bf16[784,128]{1,0:T(8,128)(2,1)S(1)}, bf16[784,128]{1,0:T(8,128)(2,1)S(1)}, u32[]{:S(2)}, u32[]{:S(2)}) collective-permute-start(bf16[784,128]{1,0:T(8,128)(2,1)S(1)} %broadcast_select_fusion.1), channel_id=1, source_target_pairs={{64,32},{128,96},{192,160},{256,224},{320,288},{384,352},{448,416}... | collective-permute-start | bytes 602120 | tf_op jit(solution)/shard_map/send_relay/ppermute | solution.py:195
  61.0 49.7 %collective-permute-start.11 = (bf16[784,128]{1,0:T(8,128)(2,1)S(1)}, bf16[784,128]{1,0:T(8,128)(2,1)S(1)}, u32[]{:S(2)}, u32[]{:S(2)}) collective-permute-start(bf16[784,128]{1,0:T(8,128)(2,1)S(1)} %collective-permute-done.9.refs_6_), channel_id=1, source_target_pairs={{32,0},{96,64},{160,128},{224,192},{288,256},{352,320},{416,384},{... | collective-permute-start | bytes 602120 | tf_op jit(solution)/shard_map/send_swap1/ppermute | solution.py:195
  62.4 48.9 %collective-permute-start.5 = (bf16[1552,128]{1,0:T(8,128)(2,1)S(1)}, bf16[1552,128]{1,0:T(8,128)(2,1)S(1)}, u32[]{:S(2)}, u32[]{:S(2)}) collective-permute-start(bf16[1552,128]{1,0:T(8,128)(2,1)S(1)} %constant_dynamic-update-slice_fusion.refs_1_), channel_id=1, source_target_pairs={{2,0},{3,1},{4,2},{5,3},{6,4},{7,5},{8,6},{9,7},{10,8},{11,9},{12,... | collective-permute-start | bytes 1191944 | tf_op jit(solution)/shard_map/send_after2/ppermute | solution.py:195
  98.6 21.2 %collective-permute-start.4 = (bf16[1552,128]{1,0:T(8,128)(2,1)S(1)}, bf16[1552,128]{1,0:T(8,128)(2,1)S(1)}, u32[]{:S(2)}, u32[]{:S(2)}) collective-permute-start(bf16[1552,128]{1,0:T(8,128)(2,1)S(1)} %constant_dynamic-update-slice_fusion.refs_1_), channel_id=1, source_target_pairs={{1,0},{2,1},{3,2},{4,3},{5,4},{6,5},{7,6},{8,7},{9,8},{10,9},{11,1... | collective-permute-start | bytes 1191944 | tf_op jit(solution)/shard_map/send_after/ppermute | solution.py:195
  100.5 24.0 %collective-permute-start.3 = (bf16[1552,128]{1,0:T(8,128)(2,1)S(1)}, bf16[1552,128]{1,0:T(8,128)(2,1)S(1)}, u32[]{:S(2)}, u32[]{:S(2)}) collective-permute-start(bf16[1552,128]{1,0:T(8,128)(2,1)S(1)} %constant_dynamic-update-slice_fusion.refs_1_), channel_id=1, source_target_pairs={{0,1},{1,2},{2,3},{3,4},{4,5},{5,6},{6,7},{7,8},{8,9},{9,10},{10,1... | collective-permute-start | bytes 1191944 | tf_op jit(solution)/shard_map/send_before/ppermute | solution.py:195
  106.7 4.5 %collective-permute-start.12 = (bf16[784,128]{1,0:T(8,128)(2,1)}, bf16[784,128]{1,0:T(8,128)(2,1)S(1)}, u32[]{:S(2)}, u32[]{:S(2)}) collective-permute-start(bf16[784,128]{1,0:T(8,128)(2,1)} %broadcast_select_fusion), channel_id=1, source_target_pairs={{32,0},{96,64},{160,128},{224,192},{288,256},{352,320},{416,384},{... | collective-permute-start | bytes 602120 | tf_op jit(solution)/shard_map/send_swap2/ppermute | solution.py:195
